TPU v7x, 32 devices: a whole 2x2x4 slice. The times are simulated.
32 devices in a mesh: problem: 2 (over y), worker: 4 (over z), head: 4 (over x, core).
Axes of the slice: x: 2, y: 2, z: 4, core: 2. Of those that a mesh axis runs over, the one named last changes fastest.
Arguments:
- queries: bfloat16 [8, 4, 40, 128], P(('problem', 'worker'), None, 'head'), parts along dimension 0, may hold values from -60 to 60
- cache_keys: bfloat16 [8, 2048, 8, 128], P(('problem', 'worker'), None, 'head'), parts along dimension 0, may hold values from -6 to 6
- cache_values: bfloat16 [8, 2048, 8, 128], P(('problem', 'worker'), None, 'head'), parts along dimension 0, may hold values from -6 to 6
- new_keys: bfloat16 [8, 4, 8, 128], P(('problem', 'worker'), None, 'head'), parts along dimension 0, may hold values from -6 to 6
- new_values: bfloat16 [8, 4, 8, 128], P(('problem', 'worker'), None, 'head'), parts along dimension 0, may hold values from -6 to 6
- lengths: int32 [8, 4], P(('problem', 'worker')), parts along dimension 0, may hold values from 1 to 2048, as said below
Outputs:
- attended: bfloat16 [8, 4, 40, 128], P(('problem', 'worker'), None, 'head'), parts along dimension 0
There are 2 independent parts, one for each index of `problem`. A program takes and returns all parts, laid end to end along the dimension named above; each array names one. Nothing has to cross between parts.
Inputs may be any that keep to these rules, and one draw needn't show every extreme that they name: lengths never fall from one step to the next; some worker's length at the last step is exactly 2048.
All inputs are finite; a program needn't handle non-finite values.
Results may differ from a plain program's by a relative error of at most 0.005.
Values may be sent and summed in bfloat16 or wider, within the bound.
No kernel may reach another device: no remote copies, remote signals or barrier semaphores. Data moves between devices by JAX's collectives and lax.ppermute only.
A program may use at most 64 MiB of HBM per device.

v0:
```python
import functools
import math

import jax
import jax.numpy as jnp
from jax import lax
from jax.experimental import pallas as pl
from jax.experimental.pallas import tpu as pltpu
from jax.sharding import PartitionSpec as P

masked_score = -1e30
lane_width = 128
stat_rows = 8


def split_heads(source_ref, wide_ref, target_ref, kv_local):
    slots, width = target_ref.shape[0], source_ref.shape[1]
    wide_ref[...] = source_ref[...].astype(jnp.float32)
    for head in range(kv_local):
        picked = wide_ref[pl.ds(head, slots, stride=kv_local), :]
        target_ref[:, pl.ds(head * width, width)] = picked.astype(jnp.bfloat16)


def place_fresh(source_ref, small_ref, pad_ref, target_ref, kv_local):
    steps = source_ref.shape[0] // kv_local
    width = source_ref.shape[1]
    begin = target_ref.shape[0] - lane_width
    small_ref[...] = source_ref[...].astype(jnp.float32)
    pad_ref[...] = jnp.zeros_like(pad_ref)
    for head in range(kv_local):
        pad_ref[pl.ds(0, steps), pl.ds(head * width, width)] = small_ref[pl.ds(head, steps, stride=kv_local), :]
    target_ref[pl.ds(begin, lane_width), :] = pad_ref[...].astype(jnp.bfloat16)


def attend_block(query_rows, lengths_ref, keys_ref, values_ref, kv_local, steps, own):
    count, (per_worker, width) = len(query_rows), query_rows[0].shape
    rows = count * per_worker
    slots = keys_ref.shape[0] - lane_width
    row = lax.broadcasted_iota(jnp.int32, (rows, 1), 0)
    step = row % steps
    head = row % per_worker // (per_worker // kv_local)
    wide = jnp.concatenate([shard.astype(jnp.float32) for shard in query_rows], axis=0)
    queries = jnp.concatenate(
        [jnp.where(head == k, wide, 0.0) for k in range(kv_local)], axis=1
    ).astype(jnp.bfloat16)
    scale = width ** (-0.5) * math.log2(math.e)
    scores = (
        lax.dot_general(
            queries, keys_ref[...], (((1,), (1,)), ((), ())), preferred_element_type=jnp.float32
        )
        * scale
    )
    limit = jnp.zeros((rows, 1), jnp.int32)
    for t in range(steps):
        limit = jnp.where(step == t, lengths_ref[0, t], limit)
    column = lax.broadcasted_iota(jnp.int32, (rows, slots), 1)
    cached = jnp.where(column < limit, scores[:, :slots], masked_score)
    fresh_limit = step + 1 if own else step
    fresh_column = lax.broadcasted_iota(jnp.int32, (rows, lane_width), 1)
    fresh = jnp.where(fresh_column < fresh_limit, scores[:, slots:], masked_score)
    top = jnp.maximum(
        jnp.max(cached, axis=1, keepdims=True), jnp.max(fresh, axis=1, keepdims=True)
    )
    top = top.astype(jnp.bfloat16).astype(jnp.float32)
    cached_weights = jnp.exp2(cached - top)
    fresh_weights = jnp.exp2(fresh - top)
    total = jnp.sum(cached_weights, axis=1, keepdims=True) + jnp.sum(
        fresh_weights, axis=1, keepdims=True
    )
    weights = jnp.concatenate(
        [cached_weights.astype(jnp.bfloat16), fresh_weights.astype(jnp.bfloat16)], axis=1
    )
    both = jnp.dot(weights, values_ref[...], preferred_element_type=jnp.float32)
    outputs = both[:, :width]
    for k in range(1, kv_local):
        outputs = jnp.where(head == k, both[:, k * width : (k + 1) * width], outputs)
    return outputs, top, total


def to_lanes(column):
    rows = column.shape[0]
    shape = (rows, lane_width)
    here = lax.broadcasted_iota(jnp.int32, shape, 0) == lax.broadcasted_iota(jnp.int32, shape, 1)
    return jnp.sum(jnp.where(here, column, 0.0), axis=0, keepdims=True)


def to_column(line, rows):
    shape = (rows, lane_width)
    here = lax.broadcasted_iota(jnp.int32, shape, 0) == lax.broadcasted_iota(jnp.int32, shape, 1)
    return jnp.sum(jnp.where(here, line, 0.0), axis=1, keepdims=True)


def pack(outputs, top, total):
    high = total.astype(jnp.bfloat16).astype(jnp.float32)
    top_line, high_line, low_line = to_lanes(top), to_lanes(high), to_lanes(total - high)
    line = lax.broadcasted_iota(jnp.int32, (stat_rows, lane_width), 0)
    stats = jnp.where(line == 0, top_line, jnp.where(line == 1, high_line, low_line))
    return jnp.concatenate([outputs, stats], axis=0).astype(jnp.bfloat16)


def first_kernel(
    kv_local, steps, chunks, lengths_ref, query_hbm, cache_keys_hbm, cache_values_hbm, new_keys_hbm,
    new_values_hbm, keys_ref, values_ref, outputs_ref, stats_ref, query_ref, raw_keys_ref, raw_values_ref,
    new_ref, wide_ref, small_ref, pad_ref, cache_sem, small_sem,
):
    size = raw_keys_ref.shape[0] // chunks
    fetch = [
        [
            pltpu.make_async_copy(
                source.at[pl.ds(i * size, size)], target.at[pl.ds(i * size, size)], cache_sem.at[side, i]
            )
            for i in range(chunks)
        ]
        for side, (source, target) in enumerate(
            ((cache_keys_hbm, raw_keys_ref), (cache_values_hbm, raw_values_ref))
        )
    ]
    small = [
        pltpu.make_async_copy(query_hbm, query_ref, small_sem.at[0]),
        pltpu.make_async_copy(new_keys_hbm, new_ref.at[0], small_sem.at[1]),
        pltpu.make_async_copy(new_values_hbm, new_ref.at[1], small_sem.at[2]),
    ]
    for copy in small + fetch[0] + fetch[1]:
        copy.start()
    for copy in small:
        copy.wait()
    place_fresh(new_ref.at[0], small_ref.at[0], pad_ref.at[0], keys_ref, kv_local)
    place_fresh(new_ref.at[1], small_ref.at[1], pad_ref.at[1], values_ref, kv_local)
    for side, (raw_ref, target_ref) in enumerate(((raw_keys_ref, keys_ref), (raw_values_ref, values_ref))):
        for i in range(chunks):
            fetch[side][i].wait()
            part = pl.ds(i * size, size)
            split_heads(
                raw_ref.at[part], wide_ref.at[side, part], target_ref.at[pl.ds(i * size // kv_local, size // kv_local)], kv_local
            )
    outputs, top, total = attend_block(
        [query_ref[...]], lengths_ref, keys_ref, values_ref, kv_local, steps, True
    )
    outputs_ref[...] = outputs
    lane = lax.broadcasted_iota(jnp.int32, stats_ref.shape, 1)
    stats_ref[...] = jnp.where(lane == 0, top, total)


def other_kernel(kv_local, steps, count, lengths_ref, *refs):
    queries, (keys_ref, values_ref), packets = refs[:count], refs[count : count + 2], refs[count + 2 :]
    rows = queries[0].shape[0]
    results = attend_block(
        [query_ref[...] for query_ref in queries], lengths_ref, keys_ref, values_ref, kv_local, steps, False
    )
    for place, packet_ref in enumerate(packets):
        packet_ref[...] = pack(*[part[place * rows : (place + 1) * rows] for part in results])


def merge_kernel(rows, outputs_ref, stats_ref, *refs):
    packets, merged_ref = refs[:-1], refs[-1]
    stats = stats_ref[...]
    parts = [(outputs_ref[...], stats[:, 0:1], stats[:, 1:2])]
    for packet_ref in packets:
        packet = packet_ref[...].astype(jnp.float32)
        lines = packet[rows : rows + stat_rows]
        parts.append(
            (
                packet[:rows],
                to_column(lines[0:1], rows),
                to_column(lines[1:2] + lines[2:3], rows),
            )
        )
    highest = functools.reduce(jnp.maximum, [top for _, top, _ in parts])
    factors = [jnp.exp2(top - highest) for _, top, _ in parts]
    total = sum(factor * part[2] for factor, part in zip(factors, parts))
    merged = sum(factor * part[0] for factor, part in zip(factors, parts))
    merged_ref[...] = (merged / total).astype(merged_ref.dtype)


vmem = pl.BlockSpec(memory_space=pltpu.VMEM)
hbm = pl.BlockSpec(memory_space=pltpu.HBM)
smem = pl.BlockSpec(memory_space=pltpu.SMEM)
grant = 40 * 1024 * 1024


def shift(shard, offset, workers):
    return lax.ppermute(shard, "worker", [(i, (i + offset) % workers) for i in range(workers)])


def local(queries, cache_keys, cache_values, new_keys, new_values, lengths):
    _, steps, heads, width = queries.shape
    slots, kv_local = cache_keys.shape[1:3]
    rows = steps * heads
    workers = lax.axis_size("worker")
    chunks = max(1, slots // 512)
    flat = lambda cache: cache.reshape(-1, width)
    as_rows = lambda q: q[0].transpose(1, 0, 2).reshape(rows, width)
    prepared = jax.ShapeDtypeStruct((slots + lane_width, kv_local * width), jnp.bfloat16)
    packet = jax.ShapeDtypeStruct((rows + stat_rows, width), jnp.bfloat16)

    def first(query_rows):
        return pl.pallas_call(
            functools.partial(first_kernel, kv_local, steps, chunks),
            out_shape=(
                prepared,
                prepared,
                jax.ShapeDtypeStruct((rows, width), jnp.float32),
                jax.ShapeDtypeStruct((rows, lane_width), jnp.float32),
            ),
            in_specs=[smem] + [hbm] * 5,
            out_specs=(vmem,) * 4,
            scratch_shapes=[
                pltpu.VMEM((rows, width), jnp.bfloat16),
                pltpu.VMEM((slots * kv_local, width), jnp.bfloat16),
                pltpu.VMEM((slots * kv_local, width), jnp.bfloat16),
                pltpu.VMEM((2, steps * kv_local, width), jnp.bfloat16),
                pltpu.VMEM((2, slots * kv_local, width), jnp.float32),
                pltpu.VMEM((2, steps * kv_local, width), jnp.float32),
                pltpu.VMEM((2, lane_width, kv_local * width), jnp.float32),
                pltpu.SemaphoreType.DMA((2, chunks)),
                pltpu.SemaphoreType.DMA((3,)),
            ],
            compiler_params=pltpu.CompilerParams(vmem_limit_bytes=grant),
            name="own_rows",
        )(lengths, query_rows, flat(cache_keys), flat(cache_values), flat(new_keys), flat(new_values))

    def others(query_list, keys, values):
        count = len(query_list)
        return pl.pallas_call(
            functools.partial(other_kernel, kv_local, steps, count),
            out_shape=(packet,) * count,
            in_specs=[smem] + [vmem] * (count + 2),
            out_specs=(vmem,) * count,
            compiler_params=pltpu.CompilerParams(vmem_limit_bytes=grant),
            name="partner_rows",
        )(lengths, *query_list, keys, values)

    def merge(outputs, stats, packets):
        return pl.pallas_call(
            functools.partial(merge_kernel, rows),
            out_shape=jax.ShapeDtypeStruct((rows, width), jnp.bfloat16),
            in_specs=[vmem] * (2 + len(packets)),
            out_specs=vmem,
            compiler_params=pltpu.CompilerParams(vmem_limit_bytes=grant // 10),
            name="merge",
        )(outputs, stats, *packets)

    arrived = [as_rows(shift(queries, offset, workers)) for offset in range(1, workers)]
    keys, values, outputs, stats = first(as_rows(queries))
    sent = others(arrived, keys, values) if arrived else ()
    packets = [shift(p, -offset, workers) for offset, p in enumerate(sent, 1)]
    merged = merge(outputs, stats, packets)
    return merged.reshape(heads, steps, width).transpose(1, 0, 2)[None]


def solution(mesh):
    split = P(("problem", "worker"), None, "head", None)
    return jax.shard_map(
        local,
        mesh=mesh,
        in_specs=(split,) * 5 + (P(("problem", "worker"), None),),
        out_specs=split,
        check_vma=False,
    )
```

profile of v0, /device:TPU:0, one launch (start us, length us, event | category | flops | bytes accessed | tf_op | source)
XLA Modules:
  0.0 24.9 jit_solution(6675939064185319931)
XLA Ops:
  0.0 3.0 %collective-permute-start = (bf16[1,4,10,128]{3,1,2,0:T(4,128)(2,1)}, bf16[1,4,10,128]{3,1,2,0:T(4,128)(2,1)S(1)}, u32[]{:S(2)}, u32[]{:S(2)}) collective-permute-start(bf16[1,4,10,128]{3,1,2,0:T(4,128)(2,1)} %param.6), channel_id=1, source_target_pairs={{0,4},{4,8},{8,12},{12,0},{1,5},{5,9},{9,13},{13,1},{2,6},{6,10},{... | collective-permute-start | bytes 30728 | tf_op jit(solution)/shard_map/ppermute | solution.py:182
  3.0 2.0 %collective-permute-start.2 = (bf16[1,4,10,128]{3,1,2,0:T(4,128)(2,1)}, bf16[1,4,10,128]{3,1,2,0:T(4,128)(2,1)S(1)}, u32[]{:S(2)}, u32[]{:S(2)}) collective-permute-start(bf16[1,4,10,128]{3,1,2,0:T(4,128)(2,1)} %param.6), channel_id=1, source_target_pairs={{0,12},{4,0},{8,4},{12,8},{1,13},{5,1},{9,5},{13,9},{2,14},{6,2},{... | collective-permute-start | bytes 30728 | tf_op jit(solution)/shard_map/ppermute | solution.py:182
  5.1 1.0 %collective-permute-start.1 = (bf16[1,4,10,128]{3,1,2,0:T(4,128)(2,1)}, bf16[1,4,10,128]{3,1,2,0:T(4,128)(2,1)S(1)}, u32[]{:S(2)}, u32[]{:S(2)}) collective-permute-start(bf16[1,4,10,128]{3,1,2,0:T(4,128)(2,1)} %param.6), channel_id=1, source_target_pairs={{0,8},{4,12},{8,0},{12,4},{1,9},{5,13},{9,1},{13,5},{2,10},{6,14},... | collective-permute-start | bytes 30728 | tf_op jit(solution)/shard_map/ppermute | solution.py:182
  6.1 0.0 copy-start
  6.1 1.2 %copy-done = bf16[1,2048,2,128]{3,2,1,0:T(2,128)(2,1)S(1)} copy-done((bf16[1,2048,2,128]{3,2,1,0:T(2,128)(2,1)S(1)}, bf16[1,2048,2,128]{3,2,1,0:T(2,128)(2,1)}, u32[]{:S(2)}) %copy-start) | copy-done | bytes 1048600
  7.3 0.0 copy-start.1
  7.3 1.2 %copy-done.1 = bf16[1,2048,2,128]{3,2,1,0:T(2,128)(2,1)S(1)} copy-done((bf16[1,2048,2,128]{3,2,1,0:T(2,128)(2,1)S(1)}, bf16[1,2048,2,128]{3,2,1,0:T(2,128)(2,1)}, u32[]{:S(2)}) %copy-start.1) | copy-done | bytes 1048600
  8.5 0.0 copy-start.2
  8.5 0.7 %copy-done.2 = bf16[1,4,10,128]{3,1,2,0:T(4,128)(2,1)S(1)} copy-done((bf16[1,4,10,128]{3,1,2,0:T(4,128)(2,1)S(1)}, bf16[1,4,10,128]{3,1,2,0:T(4,128)(2,1)}, u32[]{:S(2)}) %copy-start.2) | copy-done | bytes 10264
  9.2 0.7 %copy-done.3 = bf16[1,4,2,128]{3,2,1,0:T(2,128)(2,1)S(1)} copy-done((bf16[1,4,2,128]{3,2,1,0:T(2,128)(2,1)S(1)}, bf16[1,4,2,128]{3,2,1,0:T(2,128)(2,1)}, u32[]{:S(2)}) %copy-start.3) | copy-done | bytes 2072
  9.9 0.7 %copy-done.4 = bf16[1,4,2,128]{3,2,1,0:T(2,128)(2,1)S(1)} copy-done((bf16[1,4,2,128]{3,2,1,0:T(2,128)(2,1)S(1)}, bf16[1,4,2,128]{3,2,1,0:T(2,128)(2,1)}, u32[]{:S(2)}) %copy-start.4) | copy-done | bytes 2072
  10.6 0.7 %copy-done.5 = s32[1,4]{1,0:T(1,128)S(1)} copy-done((s32[1,4]{1,0:T(1,128)S(1)}, s32[1,4]{1,0:T(1,128)}, u32[]{:S(2)}) %copy-start.5) | copy-done | bytes 40
  11.2 2.4 %own_rows.1 = (bf16[2176,256]{1,0:T(8,128)(2,1)S(1)}, bf16[2176,256]{1,0:T(8,128)(2,1)S(1)}, f32[40,128]{1,0:T(8,128)S(1)}, f32[40,128]{1,0:T(8,128)S(1)}) custom-call(s32[1,4]{1,0:T(1,128)S(1)} %copy-done.5, bf16[40,128]{1,0:T(8,128)(2,1)S(1)} %bitcast.31, bf16[4096,128]{1,0:T(8,128)(2,1)S(1)} %bitcast.29, bf16[4096,128]{1,0:T(8,128)(2,1)S(1)} %bitcast.30, ...), custom_call_target="tpu_custom_call" | custom-call | tf_op jit(solution)/shard_map/own_rows/pallas_call | solution.py:197
  13.7 0.0 collective-permute-done
  13.7 0.0 collective-permute-done.2
  13.7 0.0 collective-permute-done.1
  13.7 1.7 %partner_rows.1 = (bf16[48,128]{1,0:T(8,128)(2,1)S(1)}, bf16[48,128]{1,0:T(8,128)(2,1)S(1)}, bf16[48,128]{1,0:T(8,128)(2,1)S(1)}) custom-call(s32[1,4]{1,0:T(1,128)S(1)} %copy-done.5, bf16[40,128]{1,0:T(8,128)(2,1)S(1)} %bitcast.32, bf16[40,128]{1,0:T(8,128)(2,1)S(1)} %bitcast.34, bf16[40,128]{1,0:T(8,128)(2,1)S(1)} %bitcast.33, ...), custom_call_target="tpu_custom_call" | custom-call | tf_op jit(solution)/shard_map/partner_rows/pallas_call | solution.py:224
  15.4 1.4 %collective-permute-start.3 = (bf16[48,128]{1,0:T(8,128)(2,1)S(1)}, bf16[48,128]{1,0:T(8,128)(2,1)S(1)}, u32[]{:S(2)}, u32[]{:S(2)}) collective-permute-start(bf16[48,128]{1,0:T(8,128)(2,1)S(1)} %get-tuple-element.16), channel_id=1, source_target_pairs={{0,12},{4,0},{8,4},{12,8},{1,13},{5,1},{9,5},{13,9},{2,14},{6,2},{... | collective-permute-start | bytes 36872 | tf_op jit(solution)/shard_map/ppermute | solution.py:182
  16.8 1.7 %collective-permute-start.4 = (bf16[48,128]{1,0:T(8,128)(2,1)S(1)}, bf16[48,128]{1,0:T(8,128)(2,1)S(1)}, u32[]{:S(2)}, u32[]{:S(2)}) collective-permute-start(bf16[48,128]{1,0:T(8,128)(2,1)S(1)} %get-tuple-element.17), channel_id=1, source_target_pairs={{0,8},{4,12},{8,0},{12,4},{1,9},{5,13},{9,1},{13,5},{2,10},{6,14},... | collective-permute-start | bytes 36872 | tf_op jit(solution)/shard_map/ppermute | solution.py:182
  18.5 0.9 %collective-permute-start.5 = (bf16[48,128]{1,0:T(8,128)(2,1)S(1)}, bf16[48,128]{1,0:T(8,128)(2,1)S(1)}, u32[]{:S(2)}, u32[]{:S(2)}) collective-permute-start(bf16[48,128]{1,0:T(8,128)(2,1)S(1)} %get-tuple-element.18), channel_id=1, source_target_pairs={{0,4},{4,8},{8,12},{12,0},{1,5},{5,9},{9,13},{13,1},{2,6},{6,10},{... | collective-permute-start | bytes 36872 | tf_op jit(solution)/shard_map/ppermute | solution.py:182
  19.4 0.0 collective-permute-done.3.refs_0_
  19.4 2.0 %collective-permute-done.4.refs_1_ = bf16[48,128]{1,0:T(8,128)(2,1)S(1)} collective-permute-done((bf16[48,128]{1,0:T(8,128)(2,1)S(1)}, bf16[48,128]{1,0:T(8,128)(2,1)S(1)}, u32[]{:S(2)}, u32[]{:S(2)}) %collective-permute-start.4) | collective-permute-done | bytes 12320 | tf_op jit(solution)/shard_map/ppermute | solution.py:182
  21.4 2.6 %collective-permute-done.5.refs_2_ = bf16[48,128]{1,0:T(8,128)(2,1)S(1)} collective-permute-done((bf16[48,128]{1,0:T(8,128)(2,1)S(1)}, bf16[48,128]{1,0:T(8,128)(2,1)S(1)}, u32[]{:S(2)}, u32[]{:S(2)}) %collective-permute-start.5) | collective-permute-done | bytes 12320 | tf_op jit(solution)/shard_map/ppermute | solution.py:182
  24.0 0.8 %merge.1 = bf16[40,128]{1,0:T(8,128)(2,1)} custom-call(f32[40,128]{1,0:T(8,128)S(1)} %get-tuple-element.12.outputs_ref, f32[40,128]{1,0:T(8,128)S(1)} %get-tuple-element.13.stats_ref, bf16[48,128]{1,0:T(8,128)(2,1)S(1)} %collective-permute-done.3.refs_0_, bf16[48,128]{1,0:T(8,128)(2,1)S(1)} %collective-permute-done.4.refs_1_, ...), custom_call_target="tpu_custom_call" | custom-call | tf_op jit(solution)/shard_map/merge/pallas_call | solution.py:234
  (3 shorter events, 0.0 us)
Async XLA Ops:
  0.0 13.7 %collective-permute-start = (bf16[1,4,10,128]{3,1,2,0:T(4,128)(2,1)}, bf16[1,4,10,128]{3,1,2,0:T(4,128)(2,1)S(1)}, u32[]{:S(2)}, u32[]{:S(2)}) collective-permute-start(bf16[1,4,10,128]{3,1,2,0:T(4,128)(2,1)} %param.6), channel_id=1, source_target_pairs={{0,4},{4,8},{8,12},{12,0},{1,5},{5,9},{9,13},{13,1},{2,6},{6,10},{... | collective-permute-start | bytes 30728 | tf_op jit(solution)/shard_map/ppermute | solution.py:182
  3.0 10.7 %collective-permute-start.2 = (bf16[1,4,10,128]{3,1,2,0:T(4,128)(2,1)}, bf16[1,4,10,128]{3,1,2,0:T(4,128)(2,1)S(1)}, u32[]{:S(2)}, u32[]{:S(2)}) collective-permute-start(bf16[1,4,10,128]{3,1,2,0:T(4,128)(2,1)} %param.6), channel_id=1, source_target_pairs={{0,12},{4,0},{8,4},{12,8},{1,13},{5,1},{9,5},{13,9},{2,14},{6,2},{... | collective-permute-start | bytes 30728 | tf_op jit(solution)/shard_map/ppermute | solution.py:182
  5.1 8.6 %collective-permute-start.1 = (bf16[1,4,10,128]{3,1,2,0:T(4,128)(2,1)}, bf16[1,4,10,128]{3,1,2,0:T(4,128)(2,1)S(1)}, u32[]{:S(2)}, u32[]{:S(2)}) collective-permute-start(bf16[1,4,10,128]{3,1,2,0:T(4,128)(2,1)} %param.6), channel_id=1, source_target_pairs={{0,8},{4,12},{8,0},{12,4},{1,9},{5,13},{9,1},{13,5},{2,10},{6,14},... | collective-permute-start | bytes 30728 | tf_op jit(solution)/shard_map/ppermute | solution.py:182
  6.1 1.2 %copy-start = (bf16[1,2048,2,128]{3,2,1,0:T(2,128)(2,1)S(1)}, bf16[1,2048,2,128]{3,2,1,0:T(2,128)(2,1)}, u32[]{:S(2)}) copy-start(bf16[1,2048,2,128]{3,2,1,0:T(2,128)(2,1)} %param.7) | copy-start | bytes 3145732
  7.3 1.2 %copy-start.1 = (bf16[1,2048,2,128]{3,2,1,0:T(2,128)(2,1)S(1)}, bf16[1,2048,2,128]{3,2,1,0:T(2,128)(2,1)}, u32[]{:S(2)}) copy-start(bf16[1,2048,2,128]{3,2,1,0:T(2,128)(2,1)} %param.8) | copy-start | bytes 3145732
  8.5 0.7 %copy-start.2 = (bf16[1,4,10,128]{3,1,2,0:T(4,128)(2,1)S(1)}, bf16[1,4,10,128]{3,1,2,0:T(4,128)(2,1)}, u32[]{:S(2)}) copy-start(bf16[1,4,10,128]{3,1,2,0:T(4,128)(2,1)} %param.6) | copy-start | bytes 30724
  9.2 0.7 %copy-start.3 = (bf16[1,4,2,128]{3,2,1,0:T(2,128)(2,1)S(1)}, bf16[1,4,2,128]{3,2,1,0:T(2,128)(2,1)}, u32[]{:S(2)}) copy-start(bf16[1,4,2,128]{3,2,1,0:T(2,128)(2,1)} %param.9) | copy-start | bytes 6148
  9.9 0.7 %copy-start.4 = (bf16[1,4,2,128]{3,2,1,0:T(2,128)(2,1)S(1)}, bf16[1,4,2,128]{3,2,1,0:T(2,128)(2,1)}, u32[]{:S(2)}) copy-start(bf16[1,4,2,128]{3,2,1,0:T(2,128)(2,1)} %param.10) | copy-start | bytes 6148
  10.6 0.7 %copy-start.5 = (s32[1,4]{1,0:T(1,128)S(1)}, s32[1,4]{1,0:T(1,128)}, u32[]{:S(2)}) copy-start(s32[1,4]{1,0:T(1,128)} %lengths_ref.3) | copy-start | bytes 52
  15.4 4.0 %collective-permute-start.3 = (bf16[48,128]{1,0:T(8,128)(2,1)S(1)}, bf16[48,128]{1,0:T(8,128)(2,1)S(1)}, u32[]{:S(2)}, u32[]{:S(2)}) collective-permute-start(bf16[48,128]{1,0:T(8,128)(2,1)S(1)} %get-tuple-element.16), channel_id=1, source_target_pairs={{0,12},{4,0},{8,4},{12,8},{1,13},{5,1},{9,5},{13,9},{2,14},{6,2},{... | collective-permute-start | bytes 36872 | tf_op jit(solution)/shard_map/ppermute | solution.py:182
  16.8 4.6 %collective-permute-start.4 = (bf16[48,128]{1,0:T(8,128)(2,1)S(1)}, bf16[48,128]{1,0:T(8,128)(2,1)S(1)}, u32[]{:S(2)}, u32[]{:S(2)}) collective-permute-start(bf16[48,128]{1,0:T(8,128)(2,1)S(1)} %get-tuple-element.17), channel_id=1, source_target_pairs={{0,8},{4,12},{8,0},{12,4},{1,9},{5,13},{9,1},{13,5},{2,10},{6,14},... | collective-permute-start | bytes 36872 | tf_op jit(solution)/shard_map/ppermute | solution.py:182
  18.5 5.5 %collective-permute-start.5 = (bf16[48,128]{1,0:T(8,128)(2,1)S(1)}, bf16[48,128]{1,0:T(8,128)(2,1)S(1)}, u32[]{:S(2)}, u32[]{:S(2)}) collective-permute-start(bf16[48,128]{1,0:T(8,128)(2,1)S(1)} %get-tuple-element.18), channel_id=1, source_target_pairs={{0,4},{4,8},{8,12},{12,0},{1,5},{5,9},{9,13},{13,1},{2,6},{6,10},{... | collective-permute-start | bytes 36872 | tf_op jit(solution)/shard_map/ppermute | solution.py:182
where the time goes:
time: 25.1 us; the launch traced here: 24.9 us
  starting transfers between devices  10.1 us (40%)
  local copies, waits for them, and re-layouts  5.17 us (21%)
  Pallas kernels  4.99 us (20%)
  waiting for transfers between devices  4.6 us (18%)
    ppermute x6, starting transfers between devices, shift(): lax.ppermute(shard, 'worker', [(i, (i + offset) % workers) for i in range...  10.1 us
    unnamed x12, local copies, waits for them, and re-layouts  5.17 us
    ppermute x6, waiting for transfers between devices, shift(): lax.ppermute(shard, 'worker', [(i, (i + offset) % workers) for i in range...  4.6 us
    pallas_call x1, Pallas kernels, first(): pl.pallas_call(functools.partial(first_kernel, kv_local, steps, chunks),...  2.43 us
    pallas_call x1, Pallas kernels, others(): pl.pallas_call(functools.partial(other_kernel, kv_local, steps, count), o...  1.72 us
    pallas_call x1, Pallas kernels, merge(): pl.pallas_call(functools.partial(merge_kernel, rows), out_shape=jax.Shape...  0.84 us
  transfers between devices with their start and end apart: 6, of which 2 were waited for; matrix products, arithmetic and copies ran while one was open for 0% of the time, Pallas kernels for 10%

commit v1 on v0

v1 whole, which is shorter than its diff:
```python
import functools
import math

import jax
import jax.numpy as jnp
from jax import lax
from jax.experimental import pallas as pl
from jax.experimental.pallas import tpu as pltpu
from jax.sharding import PartitionSpec as P

masked_score = -1e30
lane_width = 128
stat_rows = 8


def pick_head(source_ref, wide_ref, kv_local):
    slots = source_ref.shape[0] // kv_local
    wide_ref[...] = source_ref[...].astype(jnp.float32)
    return [wide_ref[pl.ds(head, slots, stride=kv_local), :] for head in range(kv_local)]


def pad_fresh(source_ref, wide_ref, pad_ref, kv_local):
    parts = pick_head(source_ref, wide_ref, kv_local)
    steps, width = parts[0].shape
    pad_ref[...] = jnp.zeros_like(pad_ref)
    for head, part in enumerate(parts):
        pad_ref[pl.ds(0, steps), pl.ds(head * width, width)] = part
    return pad_ref[...]


def widen(shards, kv_local, steps):
    count, (per_worker, width) = len(shards), shards[0].shape
    row = lax.broadcasted_iota(jnp.int32, (count * per_worker, 1), 0)
    head = row % per_worker // (per_worker // kv_local)
    rows = jnp.concatenate([shard.astype(jnp.float32) for shard in shards], axis=0)
    wide = jnp.concatenate([jnp.where(head == k, rows, 0.0) for k in range(kv_local)], axis=1)
    return wide.astype(jnp.bfloat16), row % steps, head


def score(queries, keys, limit, begin):
    scores = jnp.dot(queries, keys, preferred_element_type=jnp.float32)
    column = lax.broadcasted_iota(jnp.int32, scores.shape, 1)
    return jnp.where(column < limit - begin, scores, masked_score)


def weigh(scores, scale):
    top = functools.reduce(jnp.maximum, [jnp.max(part, axis=1, keepdims=True) for part in scores])
    top = (top * scale).astype(jnp.bfloat16).astype(jnp.float32)
    weights = [jnp.exp2(part * scale - top) for part in scores]
    total = sum(jnp.sum(part, axis=1, keepdims=True) for part in weights)
    return [part.astype(jnp.bfloat16) for part in weights], top, total


def own_columns(both, head, kv_local):
    width = both.shape[1] // kv_local
    outputs = both[:, :width]
    for k in range(1, kv_local):
        outputs = jnp.where(head == k, both[:, k * width : (k + 1) * width], outputs)
    return outputs


def to_lanes(column):
    rows = column.shape[0]
    shape = (rows, lane_width)
    here = lax.broadcasted_iota(jnp.int32, shape, 0) == lax.broadcasted_iota(jnp.int32, shape, 1)
    return jnp.sum(jnp.where(here, column, 0.0), axis=0, keepdims=True)


def to_column(line, rows):
    shape = (rows, lane_width)
    here = lax.broadcasted_iota(jnp.int32, shape, 0) == lax.broadcasted_iota(jnp.int32, shape, 1)
    return jnp.sum(jnp.where(here, line, 0.0), axis=1, keepdims=True)


def pack(outputs, top, total):
    high = total.astype(jnp.bfloat16).astype(jnp.float32)
    top_line, high_line, low_line = to_lanes(top), to_lanes(high), to_lanes(total - high)
    line = lax.broadcasted_iota(jnp.int32, (stat_rows, lane_width), 0)
    stats = jnp.where(line == 0, top_line, jnp.where(line == 1, high_line, low_line))
    return jnp.concatenate([outputs, stats], axis=0).astype(jnp.bfloat16)


def first_kernel(
    kv_local, steps, chunks, lengths_hbm, query_hbm, cache_keys_hbm, cache_values_hbm, new_keys_hbm,
    new_values_hbm, keys_ref, values_ref, limits_ref, outputs_ref, stats_ref, lengths_ref, query_ref,
    raw_keys_ref, raw_values_ref, new_ref, wide_ref, small_ref, pad_ref, cache_sem, small_sem,
):
    size = raw_keys_ref.shape[0] // chunks
    span = size // kv_local
    width = query_ref.shape[1]
    slots = values_ref.shape[0] - lane_width
    scale = width ** (-0.5) * math.log2(math.e)
    fetch = [
        [
            pltpu.make_async_copy(
                source.at[pl.ds(i * size, size)], target.at[pl.ds(i * size, size)], cache_sem.at[side, i]
            )
            for i in range(chunks)
        ]
        for side, (source, target) in enumerate(
            ((cache_keys_hbm, raw_keys_ref), (cache_values_hbm, raw_values_ref))
        )
    ]
    small = [
        pltpu.make_async_copy(lengths_hbm, lengths_ref, small_sem.at[0]),
        pltpu.make_async_copy(query_hbm, query_ref, small_sem.at[1]),
        pltpu.make_async_copy(new_keys_hbm, new_ref.at[0], small_sem.at[2]),
        pltpu.make_async_copy(new_values_hbm, new_ref.at[1], small_sem.at[3]),
    ]
    for copy in small + fetch[0] + fetch[1]:
        copy.start()
    for copy in small:
        copy.wait()
    queries, step, head = widen([query_ref[...]], kv_local, steps)
    limit = jnp.zeros(step.shape, jnp.int32)
    for t in range(steps):
        limit = jnp.where(step == t, lengths_ref[0, t], limit)
    limits_ref[...] = jnp.broadcast_to(limit, limits_ref.shape)
    fresh_keys = pad_fresh(new_ref.at[0], small_ref.at[0], pad_ref.at[0], kv_local)
    fresh_values = pad_fresh(new_ref.at[1], small_ref.at[1], pad_ref.at[1], kv_local)
    keys_ref[:, pl.ds(slots, lane_width)] = fresh_keys.T.astype(jnp.bfloat16)
    values_ref[pl.ds(slots, lane_width), :] = fresh_values.astype(jnp.bfloat16)
    scores = [score(queries, keys_ref[:, pl.ds(slots, lane_width)], step + 1, 0)]
    for i in range(chunks):
        fetch[0][i].wait()
        part, columns = pl.ds(i * size, size), pl.ds(i * span, span)
        for k, picked in enumerate(pick_head(raw_keys_ref.at[part], wide_ref.at[0, part], kv_local)):
            keys_ref[pl.ds(k * width, width), columns] = picked.T.astype(jnp.bfloat16)
        scores.append(score(queries, keys_ref[:, columns], limit, i * span))
    weights, top, total = weigh(scores, scale)
    both = jnp.dot(
        weights[0], values_ref[pl.ds(slots, lane_width), :], preferred_element_type=jnp.float32
    )
    for i in range(chunks):
        fetch[1][i].wait()
        part, lines = pl.ds(i * size, size), pl.ds(i * span, span)
        for k, picked in enumerate(pick_head(raw_values_ref.at[part], wide_ref.at[1, part], kv_local)):
            values_ref[lines, pl.ds(k * width, width)] = picked.astype(jnp.bfloat16)
        both += jnp.dot(weights[i + 1], values_ref[lines, :], preferred_element_type=jnp.float32)
    outputs_ref[...] = own_columns(both, head, kv_local)
    lane = lax.broadcasted_iota(jnp.int32, stats_ref.shape, 1)
    stats_ref[...] = jnp.where(lane == 0, top, total)


def other_kernel(kv_local, steps, count, limits_ref, *refs):
    shards, (keys_ref, values_ref), packets = refs[:count], refs[count : count + 2], refs[count + 2 :]
    rows, width = shards[0].shape
    slots = values_ref.shape[0] - lane_width
    scale = width ** (-0.5) * math.log2(math.e)
    queries, step, head = widen([shard[...] for shard in shards], kv_local, steps)
    limit = jnp.concatenate([limits_ref[:, 0:1]] * count, axis=0)
    scores = [
        score(queries, keys_ref[:, pl.ds(0, slots)], limit, 0),
        score(queries, keys_ref[:, pl.ds(slots, lane_width)], step, 0),
    ]
    weights, top, total = weigh(scores, scale)
    both = jnp.dot(
        jnp.concatenate(weights, axis=1), values_ref[...], preferred_element_type=jnp.float32
    )
    results = (own_columns(both, head, kv_local), top, total)
    for place, packet_ref in enumerate(packets):
        packet_ref[...] = pack(*[part[place * rows : (place + 1) * rows] for part in results])


def merge_kernel(rows, outputs_ref, stats_ref, *refs):
    packets, merged_ref = refs[:-1], refs[-1]
    stats = stats_ref[...]
    parts = [(outputs_ref[...], stats[:, 0:1], stats[:, 1:2])]
    for packet_ref in packets:
        packet = packet_ref[...].astype(jnp.float32)
        lines = packet[rows : rows + stat_rows]
        parts.append(
            (
                packet[:rows],
                to_column(lines[0:1], rows),
                to_column(lines[1:2] + lines[2:3], rows),
            )
        )
    highest = functools.reduce(jnp.maximum, [top for _, top, _ in parts])
    factors = [jnp.exp2(top - highest) for _, top, _ in parts]
    total = sum(factor * part[2] for factor, part in zip(factors, parts))
    merged = sum(factor * part[0] for factor, part in zip(factors, parts))
    merged_ref[...] = (merged / total).astype(merged_ref.dtype)


vmem = pl.BlockSpec(memory_space=pltpu.VMEM)
hbm = pl.BlockSpec(memory_space=pltpu.HBM)
grant = 40 * 1024 * 1024


def shift(shard, offset, workers):
    return lax.ppermute(shard, "worker", [(i, (i + offset) % workers) for i in range(workers)])


def local(queries, cache_keys, cache_values, new_keys, new_values, lengths):
    _, steps, heads, width = queries.shape
    slots, kv_local = cache_keys.shape[1:3]
    rows = steps * heads
    workers = lax.axis_size("worker")
    chunks = max(1, slots // 512)
    flat = lambda cache: cache.reshape(-1, width)
    as_rows = lambda q: q[0].transpose(1, 0, 2).reshape(rows, width)
    packet = jax.ShapeDtypeStruct((rows + stat_rows, width), jnp.bfloat16)

    def first(query_rows):
        return pl.pallas_call(
            functools.partial(first_kernel, kv_local, steps, chunks),
            out_shape=(
                jax.ShapeDtypeStruct((kv_local * width, slots + lane_width), jnp.bfloat16),
                jax.ShapeDtypeStruct((slots + lane_width, kv_local * width), jnp.bfloat16),
                jax.ShapeDtypeStruct((rows, lane_width), jnp.int32),
                jax.ShapeDtypeStruct((rows, width), jnp.float32),
                jax.ShapeDtypeStruct((rows, lane_width), jnp.float32),
            ),
            in_specs=[hbm] * 6,
            out_specs=(vmem,) * 5,
            scratch_shapes=[
                pltpu.SMEM((1, steps), jnp.int32),
                pltpu.VMEM((rows, width), jnp.bfloat16),
                pltpu.VMEM((slots * kv_local, width), jnp.bfloat16),
                pltpu.VMEM((slots * kv_local, width), jnp.bfloat16),
                pltpu.VMEM((2, steps * kv_local, width), jnp.bfloat16),
                pltpu.VMEM((2, slots * kv_local, width), jnp.float32),
                pltpu.VMEM((2, steps * kv_local, width), jnp.float32),
                pltpu.VMEM((2, lane_width, kv_local * width), jnp.float32),
                pltpu.SemaphoreType.DMA((2, chunks)),
                pltpu.SemaphoreType.DMA((4,)),
            ],
            compiler_params=pltpu.CompilerParams(vmem_limit_bytes=grant),
            name="own_rows",
        )(
            *[
                pltpu.with_memory_space_constraint(x, pltpu.HBM)
                for x in (lengths, query_rows, flat(cache_keys), flat(cache_values), flat(new_keys), flat(new_values))
            ],
        )

    def others(query_list, keys, values, limits):
        count = len(query_list)
        return pl.pallas_call(
            functools.partial(other_kernel, kv_local, steps, count),
            out_shape=(packet,) * count,
            in_specs=[vmem] * (count + 3),
            out_specs=(vmem,) * count,
            compiler_params=pltpu.CompilerParams(vmem_limit_bytes=grant),
            name="partner_rows",
        )(limits, *query_list, keys, values)

    def merge(outputs, stats, packets):
        return pl.pallas_call(
            functools.partial(merge_kernel, rows),
            out_shape=jax.ShapeDtypeStruct((rows, width), jnp.bfloat16),
            in_specs=[vmem] * (2 + len(packets)),
            out_specs=vmem,
            compiler_params=pltpu.CompilerParams(vmem_limit_bytes=grant // 10),
            name="merge",
        )(outputs, stats, *packets)

    arrived = [as_rows(shift(queries, offset, workers)) for offset in range(1, workers)]
    keys, values, limits, outputs, stats = first(as_rows(queries))
    sent = others(arrived, keys, values, limits) if arrived else ()
    packets = [shift(sent[workers - 1 - offset], offset, workers) for offset in range(1, workers)]
    merged = merge(outputs, stats, packets)
    return merged.reshape(heads, steps, width).transpose(1, 0, 2)[None]


def solution(mesh):
    split = P(("problem", "worker"), None, "head", None)
    return jax.shard_map(
        local,
        mesh=mesh,
        in_specs=(split,) * 5 + (P(("problem", "worker"), None),),
        out_specs=split,
        check_vma=False,
    )
```

time: 25.1 us -> 18.2 us (0.73)
  local copies, waits for them, and re-layouts: 5.17 us -> 0 us
  waiting for transfers between devices: 4.6 us -> 1.64 us
  starting transfers between devices: 10.1 us -> 10.9 us
  Pallas kernels: 4.99 us -> 5.5 us
    unnamed x12 -> x0, local copies, waits for them, and re-layouts: 5.17 us -> none
    ppermute x6, waiting for transfers between devices: 4.6 us -> 1.64 us  [shift(): lax.ppermute(shard, 'worker', [(i, (i + offset) % workers) for i in range...]
    pallas_call x1, Pallas kernels: 2.43 us -> 3.64 us  [first(): pl.pallas_call(functools.partial(first_kernel, kv_local, steps, chunks),...]
    ppermute x6, starting transfers between devices: 10.1 us -> 10.9 us  [shift(): lax.ppermute(shard, 'worker', [(i, (i + offset) % workers) for i in range...]
    pallas_call x1, Pallas kernels: 1.72 us -> 1.02 us  [others(): pl.pallas_call(functools.partial(other_kernel, kv_local, steps, count), o...]
  transfers between devices with their start and end apart: 6 -> 6, of which waited for: 2 -> 4; matrix products, arithmetic and copies ran while one was open for 0% -> 0% of each run, Pallas kernels for 10% -> 20%
where the time goes in v1:
time: 18.2 us; the launch traced here: 18 us
  starting transfers between devices  10.9 us (60%)
  Pallas kernels  5.5 us (30%)
  waiting for transfers between devices  1.64 us (9%)
    ppermute x6, starting transfers between devices, shift(): lax.ppermute(shard, 'worker', [(i, (i + offset) % workers) for i in range...  10.9 us
    pallas_call x1, Pallas kernels, first(): pl.pallas_call(functools.partial(first_kernel, kv_local, steps, chunks),...  3.64 us
    ppermute x6, waiting for transfers between devices, shift(): lax.ppermute(shard, 'worker', [(i, (i + offset) % workers) for i in range...  1.64 us
    pallas_call x1, Pallas kernels, others(): pl.pallas_call(functools.partial(other_kernel, kv_local, steps, count), o...  1.02 us
    pallas_call x1, Pallas kernels, merge(): pl.pallas_call(functools.partial(merge_kernel, rows), out_shape=jax.Shape...  0.84 us
  transfers between devices with their start and end apart: 6, of which 4 were waited for; matrix products, arithmetic and copies ran while one was open for 0% of the time, Pallas kernels for 20%

profile of v1, /device:TPU:0, one launch (start us, length us, event | category | flops | bytes accessed | tf_op | source)
XLA Modules:
  0.0 18.0 jit_solution(13809290669718846516)
XLA Ops:
  0.0 3.0 %collective-permute-start = (bf16[1,4,10,128]{3,1,2,0:T(4,128)(2,1)}, bf16[1,4,10,128]{3,1,2,0:T(4,128)(2,1)S(1)}, u32[]{:S(2)}, u32[]{:S(2)}) collective-permute-start(bf16[1,4,10,128]{3,1,2,0:T(4,128)(2,1)} %param.6), channel_id=1, source_target_pairs={{0,4},{4,8},{8,12},{12,0},{1,5},{5,9},{9,13},{13,1},{2,6},{6,10},{... | collective-permute-start | bytes 30728 | tf_op jit(solution)/shard_map/ppermute | solution.py:192
  3.0 2.0 %collective-permute-start.2 = (bf16[1,4,10,128]{3,1,2,0:T(4,128)(2,1)}, bf16[1,4,10,128]{3,1,2,0:T(4,128)(2,1)S(1)}, u32[]{:S(2)}, u32[]{:S(2)}) collective-permute-start(bf16[1,4,10,128]{3,1,2,0:T(4,128)(2,1)} %param.6), channel_id=1, source_target_pairs={{0,12},{4,0},{8,4},{12,8},{1,13},{5,1},{9,5},{13,9},{2,14},{6,2},{... | collective-permute-start | bytes 30728 | tf_op jit(solution)/shard_map/ppermute | solution.py:192
  5.1 1.0 %collective-permute-start.1 = (bf16[1,4,10,128]{3,1,2,0:T(4,128)(2,1)}, bf16[1,4,10,128]{3,1,2,0:T(4,128)(2,1)S(1)}, u32[]{:S(2)}, u32[]{:S(2)}) collective-permute-start(bf16[1,4,10,128]{3,1,2,0:T(4,128)(2,1)} %param.6), channel_id=1, source_target_pairs={{0,8},{4,12},{8,0},{12,4},{1,9},{5,13},{9,1},{13,5},{2,10},{6,14},... | collective-permute-start | bytes 30728 | tf_op jit(solution)/shard_map/ppermute | solution.py:192
  6.1 3.6 %own_rows.1 = (bf16[256,2176]{1,0:T(8,128)(2,1)S(1)}, bf16[2176,256]{1,0:T(8,128)(2,1)S(1)}, s32[40,128]{1,0:T(8,128)S(1)}, f32[40,128]{1,0:T(8,128)S(1)}, f32[40,128]{1,0:T(8,128)S(1)}) custom-call(s32[1,4]{1,0:T(1,128)} %lengths_hbm.1, bf16[40,128]{1,0:T(8,128)(2,1)} %bitcast.34, bf16[4096,128]{1,0:T(8,128)(2,1)} %bitcast.32, bf16[4096,128]{1,0:T(8,128)(2,1)} %bitcast.33, ...), custom_call_target="tpu_custom_call" | custom-call | tf_op jit(solution)/shard_map/own_rows/pallas_call | solution.py:206
  9.7 0.0 collective-permute-done
  9.7 0.0 collective-permute-done.2
  9.7 0.1 collective-permute-done.1
  9.8 1.0 %partner_rows.1 = (bf16[48,128]{1,0:T(8,128)(2,1)S(1)}, bf16[48,128]{1,0:T(8,128)(2,1)S(1)}, bf16[48,128]{1,0:T(8,128)(2,1)S(1)}) custom-call(s32[40,128]{1,0:T(8,128)S(1)} %get-tuple-element.15.limits_ref, bf16[40,128]{1,0:T(8,128)(2,1)S(1)} %bitcast.29, bf16[40,128]{1,0:T(8,128)(2,1)S(1)} %bitcast.31, bf16[40,128]{1,0:T(8,128)(2,1)S(1)} %bitcast.30, ...), custom_call_target="tpu_custom_call" | custom-call | tf_op jit(solution)/shard_map/partner_rows/pallas_call | solution.py:240
  10.9 1.5 %collective-permute-start.3 = (bf16[48,128]{1,0:T(8,128)(2,1)S(1)}, bf16[48,128]{1,0:T(8,128)(2,1)S(1)}, u32[]{:S(2)}, u32[]{:S(2)}) collective-permute-start(bf16[48,128]{1,0:T(8,128)(2,1)S(1)} %get-tuple-element.18), channel_id=1, source_target_pairs={{0,4},{4,8},{8,12},{12,0},{1,5},{5,9},{9,13},{13,1},{2,6},{6,10},{... | collective-permute-start | bytes 36872 | tf_op jit(solution)/shard_map/ppermute | solution.py:192
  12.4 1.1 %collective-permute-start.4 = (bf16[48,128]{1,0:T(8,128)(2,1)S(1)}, bf16[48,128]{1,0:T(8,128)(2,1)S(1)}, u32[]{:S(2)}, u32[]{:S(2)}) collective-permute-start(bf16[48,128]{1,0:T(8,128)(2,1)S(1)} %get-tuple-element.19), channel_id=1, source_target_pairs={{0,8},{4,12},{8,0},{12,4},{1,9},{5,13},{9,1},{13,5},{2,10},{6,14},... | collective-permute-start | bytes 36872 | tf_op jit(solution)/shard_map/ppermute | solution.py:192
  13.5 2.2 %collective-permute-start.5 = (bf16[48,128]{1,0:T(8,128)(2,1)S(1)}, bf16[48,128]{1,0:T(8,128)(2,1)S(1)}, u32[]{:S(2)}, u32[]{:S(2)}) collective-permute-start(bf16[48,128]{1,0:T(8,128)(2,1)S(1)} %get-tuple-element.20), channel_id=1, source_target_pairs={{0,12},{4,0},{8,4},{12,8},{1,13},{5,1},{9,5},{13,9},{2,14},{6,2},{... | collective-permute-start | bytes 36872 | tf_op jit(solution)/shard_map/ppermute | solution.py:192
  15.7 0.7 %collective-permute-done.3.refs_0_ = bf16[48,128]{1,0:T(8,128)(2,1)S(1)} collective-permute-done((bf16[48,128]{1,0:T(8,128)(2,1)S(1)}, bf16[48,128]{1,0:T(8,128)(2,1)S(1)}, u32[]{:S(2)}, u32[]{:S(2)}) %collective-permute-start.3) | collective-permute-done | bytes 12320 | tf_op jit(solution)/shard_map/ppermute | solution.py:192
  16.4 0.6 %collective-permute-done.4.refs_1_ = bf16[48,128]{1,0:T(8,128)(2,1)S(1)} collective-permute-done((bf16[48,128]{1,0:T(8,128)(2,1)S(1)}, bf16[48,128]{1,0:T(8,128)(2,1)S(1)}, u32[]{:S(2)}, u32[]{:S(2)}) %collective-permute-start.4) | collective-permute-done | bytes 12320 | tf_op jit(solution)/shard_map/ppermute | solution.py:192
  17.0 0.2 %collective-permute-done.5.refs_2_ = bf16[48,128]{1,0:T(8,128)(2,1)S(1)} collective-permute-done((bf16[48,128]{1,0:T(8,128)(2,1)S(1)}, bf16[48,128]{1,0:T(8,128)(2,1)S(1)}, u32[]{:S(2)}, u32[]{:S(2)}) %collective-permute-start.5) | collective-permute-done | bytes 12320 | tf_op jit(solution)/shard_map/ppermute | solution.py:192
  17.2 0.8 %merge.1 = bf16[40,128]{1,0:T(8,128)(2,1)} custom-call(f32[40,128]{1,0:T(8,128)S(1)} %get-tuple-element.13.outputs_ref, f32[40,128]{1,0:T(8,128)S(1)} %get-tuple-element.14.stats_ref, bf16[48,128]{1,0:T(8,128)(2,1)S(1)} %collective-permute-done.3.refs_0_, bf16[48,128]{1,0:T(8,128)(2,1)S(1)} %collective-permute-done.4.refs_1_, ...), custom_call_target="tpu_custom_call" | custom-call | tf_op jit(solution)/shard_map/merge/pallas_call | solution.py:250
Async XLA Ops:
  0.0 9.7 %collective-permute-start = (bf16[1,4,10,128]{3,1,2,0:T(4,128)(2,1)}, bf16[1,4,10,128]{3,1,2,0:T(4,128)(2,1)S(1)}, u32[]{:S(2)}, u32[]{:S(2)}) collective-permute-start(bf16[1,4,10,128]{3,1,2,0:T(4,128)(2,1)} %param.6), channel_id=1, source_target_pairs={{0,4},{4,8},{8,12},{12,0},{1,5},{5,9},{9,13},{13,1},{2,6},{6,10},{... | collective-permute-start | bytes 30728 | tf_op jit(solution)/shard_map/ppermute | solution.py:192
  3.0 6.7 %collective-permute-start.2 = (bf16[1,4,10,128]{3,1,2,0:T(4,128)(2,1)}, bf16[1,4,10,128]{3,1,2,0:T(4,128)(2,1)S(1)}, u32[]{:S(2)}, u32[]{:S(2)}) collective-permute-start(bf16[1,4,10,128]{3,1,2,0:T(4,128)(2,1)} %param.6), channel_id=1, source_target_pairs={{0,12},{4,0},{8,4},{12,8},{1,13},{5,1},{9,5},{13,9},{2,14},{6,2},{... | collective-permute-start | bytes 30728 | tf_op jit(solution)/shard_map/ppermute | solution.py:192
  5.1 4.8 %collective-permute-start.1 = (bf16[1,4,10,128]{3,1,2,0:T(4,128)(2,1)}, bf16[1,4,10,128]{3,1,2,0:T(4,128)(2,1)S(1)}, u32[]{:S(2)}, u32[]{:S(2)}) collective-permute-start(bf16[1,4,10,128]{3,1,2,0:T(4,128)(2,1)} %param.6), channel_id=1, source_target_pairs={{0,8},{4,12},{8,0},{12,4},{1,9},{5,13},{9,1},{13,5},{2,10},{6,14},... | collective-permute-start | bytes 30728 | tf_op jit(solution)/shard_map/ppermute | solution.py:192
  10.9 5.5 %collective-permute-start.3 = (bf16[48,128]{1,0:T(8,128)(2,1)S(1)}, bf16[48,128]{1,0:T(8,128)(2,1)S(1)}, u32[]{:S(2)}, u32[]{:S(2)}) collective-permute-start(bf16[48,128]{1,0:T(8,128)(2,1)S(1)} %get-tuple-element.18), channel_id=1, source_target_pairs={{0,4},{4,8},{8,12},{12,0},{1,5},{5,9},{9,13},{13,1},{2,6},{6,10},{... | collective-permute-start | bytes 36872 | tf_op jit(solution)/shard_map/ppermute | solution.py:192
  12.4 4.6 %collective-permute-start.4 = (bf16[48,128]{1,0:T(8,128)(2,1)S(1)}, bf16[48,128]{1,0:T(8,128)(2,1)S(1)}, u32[]{:S(2)}, u32[]{:S(2)}) collective-permute-start(bf16[48,128]{1,0:T(8,128)(2,1)S(1)} %get-tuple-element.19), channel_id=1, source_target_pairs={{0,8},{4,12},{8,0},{12,4},{1,9},{5,13},{9,1},{13,5},{2,10},{6,14},... | collective-permute-start | bytes 36872 | tf_op jit(solution)/shard_map/ppermute | solution.py:192
  13.5 3.7 %collective-permute-start.5 = (bf16[48,128]{1,0:T(8,128)(2,1)S(1)}, bf16[48,128]{1,0:T(8,128)(2,1)S(1)}, u32[]{:S(2)}, u32[]{:S(2)}) collective-permute-start(bf16[48,128]{1,0:T(8,128)(2,1)S(1)} %get-tuple-element.20), channel_id=1, source_target_pairs={{0,12},{4,0},{8,4},{12,8},{1,13},{5,1},{9,5},{13,9},{2,14},{6,2},{... | collective-permute-start | bytes 36872 | tf_op jit(solution)/shard_map/ppermute | solution.py:192

commit v2 on v1

--- a/solution.py
+++ b/solution.py
@@ -37,10 +37,10 @@
     return wide.astype(jnp.bfloat16), row % steps, head
 
 
-def score(queries, keys, limit, begin):
+def score(queries, keys, limit):
     scores = jnp.dot(queries, keys, preferred_element_type=jnp.float32)
     column = lax.broadcasted_iota(jnp.int32, scores.shape, 1)
-    return jnp.where(column < limit - begin, scores, masked_score)
+    return jnp.where(column < limit, scores, masked_score)
 
 
 def weigh(scores, scale):
@@ -80,16 +80,15 @@
     return jnp.concatenate([outputs, stats], axis=0).astype(jnp.bfloat16)
 
 
-def first_kernel(
-    kv_local, steps, chunks, lengths_hbm, query_hbm, cache_keys_hbm, cache_values_hbm, new_keys_hbm,
-    new_values_hbm, keys_ref, values_ref, limits_ref, outputs_ref, stats_ref, lengths_ref, query_ref,
-    raw_keys_ref, raw_values_ref, new_ref, wide_ref, small_ref, pad_ref, cache_sem, small_sem,
+def prepare_kernel(
+    kv_local, steps, chunks, lengths_hbm, cache_keys_hbm, cache_values_hbm, new_keys_hbm, new_values_hbm,
+    keys_ref, values_ref, limits_ref, lengths_ref, raw_keys_ref, raw_values_ref, new_ref, wide_ref,
+    small_ref, pad_ref, cache_sem, small_sem,
 ):
     size = raw_keys_ref.shape[0] // chunks
     span = size // kv_local
-    width = query_ref.shape[1]
+    width = raw_keys_ref.shape[1]
     slots = values_ref.shape[0] - lane_width
-    scale = width ** (-0.5) * math.log2(math.e)
     fetch = [
         [
             pltpu.make_async_copy(
@@ -103,61 +102,72 @@
     ]
     small = [
         pltpu.make_async_copy(lengths_hbm, lengths_ref, small_sem.at[0]),
-        pltpu.make_async_copy(query_hbm, query_ref, small_sem.at[1]),
-        pltpu.make_async_copy(new_keys_hbm, new_ref.at[0], small_sem.at[2]),
-        pltpu.make_async_copy(new_values_hbm, new_ref.at[1], small_sem.at[3]),
+        pltpu.make_async_copy(new_keys_hbm, new_ref.at[0], small_sem.at[1]),
+        pltpu.make_async_copy(new_values_hbm, new_ref.at[1], small_sem.at[2]),
     ]
     for copy in small + fetch[0] + fetch[1]:
         copy.start()
     for copy in small:
         copy.wait()
-    queries, step, head = widen([query_ref[...]], kv_local, steps)
+    step = lax.broadcasted_iota(jnp.int32, limits_ref.shape, 0) % steps
     limit = jnp.zeros(step.shape, jnp.int32)
     for t in range(steps):
         limit = jnp.where(step == t, lengths_ref[0, t], limit)
-    limits_ref[...] = jnp.broadcast_to(limit, limits_ref.shape)
+    limits_ref[...] = limit
     fresh_keys = pad_fresh(new_ref.at[0], small_ref.at[0], pad_ref.at[0], kv_local)
     fresh_values = pad_fresh(new_ref.at[1], small_ref.at[1], pad_ref.at[1], kv_local)
-    keys_ref[:, pl.ds(slots, lane_width)] = fresh_keys.T.astype(jnp.bfloat16)
+    keys_ref[:, pl.ds(slots, lane_width)] = fresh_keys.astype(jnp.bfloat16).T
     values_ref[pl.ds(slots, lane_width), :] = fresh_values.astype(jnp.bfloat16)
-    scores = [score(queries, keys_ref[:, pl.ds(slots, lane_width)], step + 1, 0)]
     for i in range(chunks):
         fetch[0][i].wait()
         part, columns = pl.ds(i * size, size), pl.ds(i * span, span)
         for k, picked in enumerate(pick_head(raw_keys_ref.at[part], wide_ref.at[0, part], kv_local)):
-            keys_ref[pl.ds(k * width, width), columns] = picked.T.astype(jnp.bfloat16)
-        scores.append(score(queries, keys_ref[:, columns], limit, i * span))
-    weights, top, total = weigh(scores, scale)
-    both = jnp.dot(
-        weights[0], values_ref[pl.ds(slots, lane_width), :], preferred_element_type=jnp.float32
-    )
+            keys_ref[pl.ds(k * width, width), columns] = picked.astype(jnp.bfloat16).T
     for i in range(chunks):
         fetch[1][i].wait()
         part, lines = pl.ds(i * size, size), pl.ds(i * span, span)
         for k, picked in enumerate(pick_head(raw_values_ref.at[part], wide_ref.at[1, part], kv_local)):
             values_ref[lines, pl.ds(k * width, width)] = picked.astype(jnp.bfloat16)
-        both += jnp.dot(weights[i + 1], values_ref[lines, :], preferred_element_type=jnp.float32)
-    outputs_ref[...] = own_columns(both, head, kv_local)
+
+
+def attend(shards, keys_ref, values_ref, limits_ref, kv_local, steps, own):
+    count, width = len(shards), shards[0].shape[1]
+    slots = values_ref.shape[0] - lane_width
+    scale = width ** (-0.5) * math.log2(math.e)
+    queries, step, head = widen(shards, kv_local, steps)
+    limit = jnp.concatenate([limits_ref[:, 0:1]] * count, axis=0)
+    scores = [
+        score(queries, keys_ref[:, pl.ds(0, slots)], limit),
+        score(queries, keys_ref[:, pl.ds(slots, lane_width)], step + 1 if own else step),
+    ]
+    weights, top, total = weigh(scores, scale)
+    begins = (0, slots)
+    outputs = None
+    for k in range(kv_local):
+        columns = pl.ds(k * width, width)
+        part = sum(
+            jnp.dot(part, values_ref[pl.ds(begin, part.shape[1]), columns], preferred_element_type=jnp.float32)
+            for part, begin in zip(weights, begins)
+        )
+        outputs = part if outputs is None else jnp.where(head == k, part, outputs)
+    return outputs, top, total
+
+
+def own_kernel(kv_local, steps, keys_ref, values_ref, limits_ref, query_ref, outputs_ref, stats_ref):
+    outputs, top, total = attend(
+        [query_ref[...]], keys_ref, values_ref, limits_ref, kv_local, steps, True
+    )
+    outputs_ref[...] = outputs
     lane = lax.broadcasted_iota(jnp.int32, stats_ref.shape, 1)
     stats_ref[...] = jnp.where(lane == 0, top, total)
 
 
-def other_kernel(kv_local, steps, count, limits_ref, *refs):
-    shards, (keys_ref, values_ref), packets = refs[:count], refs[count : count + 2], refs[count + 2 :]
-    rows, width = shards[0].shape
-    slots = values_ref.shape[0] - lane_width
-    scale = width ** (-0.5) * math.log2(math.e)
-    queries, step, head = widen([shard[...] for shard in shards], kv_local, steps)
-    limit = jnp.concatenate([limits_ref[:, 0:1]] * count, axis=0)
-    scores = [
-        score(queries, keys_ref[:, pl.ds(0, slots)], limit, 0),
-        score(queries, keys_ref[:, pl.ds(slots, lane_width)], step, 0),
-    ]
-    weights, top, total = weigh(scores, scale)
-    both = jnp.dot(
-        jnp.concatenate(weights, axis=1), values_ref[...], preferred_element_type=jnp.float32
+def partner_kernel(kv_local, steps, count, keys_ref, values_ref, limits_ref, *refs):
+    shards, packets = refs[:count], refs[count:]
+    rows = shards[0].shape[0]
+    results = attend(
+        [shard[...] for shard in shards], keys_ref, values_ref, limits_ref, kv_local, steps, False
     )
-    results = (own_columns(both, head, kv_local), top, total)
     for place, packet_ref in enumerate(packets):
         packet_ref[...] = pack(*[part[place * rows : (place + 1) * rows] for part in results])
 
@@ -197,26 +207,23 @@
     slots, kv_local = cache_keys.shape[1:3]
     rows = steps * heads
     workers = lax.axis_size("worker")
-    chunks = max(1, slots // 512)
+    chunks = max(1, slots // 1024)
     flat = lambda cache: cache.reshape(-1, width)
     as_rows = lambda q: q[0].transpose(1, 0, 2).reshape(rows, width)
     packet = jax.ShapeDtypeStruct((rows + stat_rows, width), jnp.bfloat16)
 
-    def first(query_rows):
-        return pl.pallas_call(
-            functools.partial(first_kernel, kv_local, steps, chunks),
+    def prepare():
+        return pl.pallas_call(
+            functools.partial(prepare_kernel, kv_local, steps, chunks),
             out_shape=(
                 jax.ShapeDtypeStruct((kv_local * width, slots + lane_width), jnp.bfloat16),
                 jax.ShapeDtypeStruct((slots + lane_width, kv_local * width), jnp.bfloat16),
                 jax.ShapeDtypeStruct((rows, lane_width), jnp.int32),
-                jax.ShapeDtypeStruct((rows, width), jnp.float32),
-                jax.ShapeDtypeStruct((rows, lane_width), jnp.float32),
             ),
-            in_specs=[hbm] * 6,
-            out_specs=(vmem,) * 5,
+            in_specs=[hbm] * 5,
+            out_specs=(vmem,) * 3,
             scratch_shapes=[
                 pltpu.SMEM((1, steps), jnp.int32),
-                pltpu.VMEM((rows, width), jnp.bfloat16),
                 pltpu.VMEM((slots * kv_local, width), jnp.bfloat16),
                 pltpu.VMEM((slots * kv_local, width), jnp.bfloat16),
                 pltpu.VMEM((2, steps * kv_local, width), jnp.bfloat16),
@@ -224,27 +231,40 @@
                 pltpu.VMEM((2, steps * kv_local, width), jnp.float32),
                 pltpu.VMEM((2, lane_width, kv_local * width), jnp.float32),
                 pltpu.SemaphoreType.DMA((2, chunks)),
-                pltpu.SemaphoreType.DMA((4,)),
+                pltpu.SemaphoreType.DMA((3,)),
             ],
             compiler_params=pltpu.CompilerParams(vmem_limit_bytes=grant),
-            name="own_rows",
+            name="prepare",
         )(
             *[
                 pltpu.with_memory_space_constraint(x, pltpu.HBM)
-                for x in (lengths, query_rows, flat(cache_keys), flat(cache_values), flat(new_keys), flat(new_values))
-            ],
-        )
-
-    def others(query_list, keys, values, limits):
+                for x in (lengths, flat(cache_keys), flat(cache_values), flat(new_keys), flat(new_values))
+            ]
+        )
+
+    def own(prepared, query_rows):
+        return pl.pallas_call(
+            functools.partial(own_kernel, kv_local, steps),
+            out_shape=(
+                jax.ShapeDtypeStruct((rows, width), jnp.float32),
+                jax.ShapeDtypeStruct((rows, lane_width), jnp.float32),
+            ),
+            in_specs=[vmem] * 4,
+            out_specs=(vmem,) * 2,
+            compiler_params=pltpu.CompilerParams(vmem_limit_bytes=grant),
+            name="own_rows",
+        )(*prepared, query_rows)
+
+    def partners(prepared, query_list):
         count = len(query_list)
         return pl.pallas_call(
-            functools.partial(other_kernel, kv_local, steps, count),
+            functools.partial(partner_kernel, kv_local, steps, count),
             out_shape=(packet,) * count,
             in_specs=[vmem] * (count + 3),
             out_specs=(vmem,) * count,
             compiler_params=pltpu.CompilerParams(vmem_limit_bytes=grant),
             name="partner_rows",
-        )(limits, *query_list, keys, values)
+        )(*prepared, *query_list)
 
     def merge(outputs, stats, packets):
         return pl.pallas_call(
@@ -256,10 +276,13 @@
             name="merge",
         )(outputs, stats, *packets)
 
-    arrived = [as_rows(shift(queries, offset, workers)) for offset in range(1, workers)]
-    keys, values, limits, outputs, stats = first(as_rows(queries))
-    sent = others(arrived, keys, values, limits) if arrived else ()
-    packets = [shift(sent[workers - 1 - offset], offset, workers) for offset in range(1, workers)]
+    middle = workers // 2
+    offsets = [middle] + [offset for offset in range(1, workers) if offset != middle]
+    arrived = [as_rows(shift(queries, offset, workers)) for offset in offsets]
+    prepared = prepare()
+    sent = partners(prepared, arrived) if arrived else ()
+    packets = [shift(sent[offsets.index(workers - offset)], offset, workers) for offset in range(1, workers)]
+    outputs, stats = own(prepared, as_rows(queries))
     merged = merge(outputs, stats, packets)
     return merged.reshape(heads, steps, width).transpose(1, 0, 2)[None]
 

time: 18.2 us -> 18.1 us (level)
  waiting for transfers between devices: 1.64 us -> 3.29 us
  Pallas kernels: 5.5 us -> 4.6 us
  starting transfers between devices: 10.9 us -> 10 us
    ppermute x6, waiting for transfers between devices: 1.64 us -> 3.29 us  [shift(): lax.ppermute(shard, 'worker', [(i, (i + offset) % workers) for i in range...]
    pallas_call x2 -> x3, Pallas kernels: 4.66 us -> 3.76 us  [the longest x1 2.08 us: prepare(): pl.pallas_call(functools.partial(prepare_kernel, kv_local, steps, chunks)...]
    ppermute x6, starting transfers between devices: 10.9 us -> 10 us  [shift(): lax.ppermute(shard, 'worker', [(i, (i + offset) % workers) for i in range...]
  transfers between devices with their start and end apart: 6 -> 6, of which waited for: 4 -> 3; matrix products, arithmetic and copies ran while one was open for 0% -> 0% of each run, Pallas kernels for 20% -> 15%
where the time goes in v2:
time: 18.1 us; the launch traced here: 18 us
  starting transfers between devices  10 us (55%)
  Pallas kernels  4.6 us (25%)
  waiting for transfers between devices  3.29 us (18%)
    ppermute x6, starting transfers between devices, shift(): lax.ppermute(shard, 'worker', [(i, (i + offset) % workers) for i in range...  10 us
    ppermute x6, waiting for transfers between devices, shift(): lax.ppermute(shard, 'worker', [(i, (i + offset) % workers) for i in range...  3.29 us
    pallas_call x1, Pallas kernels, prepare(): pl.pallas_call(functools.partial(prepare_kernel, kv_local, steps, chunks)...  2.08 us
    pallas_call x1, Pallas kernels, partners(): pl.pallas_call(functools.partial(partner_kernel, kv_local, steps, count),...  0.97 us
    pallas_call x1, Pallas kernels, merge(): pl.pallas_call(functools.partial(merge_kernel, rows), out_shape=jax.Shape...  0.84 us
    pallas_call x1, Pallas kernels, own(): pl.pallas_call(functools.partial(own_kernel, kv_local, steps), out_shape=...  0.71 us
  transfers between devices with their start and end apart: 6, of which 3 were waited for; matrix products, arithmetic and copies ran while one was open for 0% of the time, Pallas kernels for 15%

profile of v2, /device:TPU:0, one launch (start us, length us, event | category | flops | bytes accessed | tf_op | source)
XLA Modules:
  0.0 18.0 jit_solution(7858391869823123309)
XLA Ops:
  0.0 3.0 %collective-permute-start.1 = (bf16[1,4,10,128]{3,1,2,0:T(4,128)(2,1)}, bf16[1,4,10,128]{3,1,2,0:T(4,128)(2,1)S(1)}, u32[]{:S(2)}, u32[]{:S(2)}) collective-permute-start(bf16[1,4,10,128]{3,1,2,0:T(4,128)(2,1)} %param.6), channel_id=1, source_target_pairs={{0,4},{4,8},{8,12},{12,0},{1,5},{5,9},{9,13},{13,1},{2,6},{6,10},{... | collective-permute-start | bytes 30728 | tf_op jit(solution)/shard_map/ppermute | solution.py:202
  3.0 2.0 %collective-permute-start.2 = (bf16[1,4,10,128]{3,1,2,0:T(4,128)(2,1)}, bf16[1,4,10,128]{3,1,2,0:T(4,128)(2,1)S(1)}, u32[]{:S(2)}, u32[]{:S(2)}) collective-permute-start(bf16[1,4,10,128]{3,1,2,0:T(4,128)(2,1)} %param.6), channel_id=1, source_target_pairs={{0,12},{4,0},{8,4},{12,8},{1,13},{5,1},{9,5},{13,9},{2,14},{6,2},{... | collective-permute-start | bytes 30728 | tf_op jit(solution)/shard_map/ppermute | solution.py:202
  5.1 1.0 %collective-permute-start = (bf16[1,4,10,128]{3,1,2,0:T(4,128)(2,1)}, bf16[1,4,10,128]{3,1,2,0:T(4,128)(2,1)S(1)}, u32[]{:S(2)}, u32[]{:S(2)}) collective-permute-start(bf16[1,4,10,128]{3,1,2,0:T(4,128)(2,1)} %param.6), channel_id=1, source_target_pairs={{0,8},{4,12},{8,0},{12,4},{1,9},{5,13},{9,1},{13,5},{2,10},{6,14},... | collective-permute-start | bytes 30728 | tf_op jit(solution)/shard_map/ppermute | solution.py:202
  6.1 2.1 %prepare.1 = (bf16[256,2176]{1,0:T(8,128)(2,1)S(1)}, bf16[2176,256]{1,0:T(8,128)(2,1)S(1)}, s32[40,128]{1,0:T(8,128)S(1)}) custom-call(s32[1,4]{1,0:T(1,128)} %lengths_hbm.1, bf16[4096,128]{1,0:T(8,128)(2,1)} %bitcast.33, bf16[4096,128]{1,0:T(8,128)(2,1)} %bitcast.34, bf16[8,128]{1,0:T(8,128)(2,1)} %bitcast.35, bf16[8,128]{1,0:T(8,128)(2,1)} %bitcast.36), custom_call_target="tpu_custom_call" | custom-call | tf_op jit(solution)/shard_map/prepare/pallas_call | solution.py:216
  8.2 0.0 collective-permute-done.1
  8.2 0.0 collective-permute-done.2
  8.2 1.7 %collective-permute-done = bf16[1,4,10,128]{3,1,2,0:T(4,128)(2,1)S(1)} collective-permute-done((bf16[1,4,10,128]{3,1,2,0:T(4,128)(2,1)}, bf16[1,4,10,128]{3,1,2,0:T(4,128)(2,1)S(1)}, u32[]{:S(2)}, u32[]{:S(2)}) %collective-permute-start) | collective-permute-done | bytes 10272 | tf_op jit(solution)/shard_map/ppermute | solution.py:202
  9.8 0.0 copy-start
  9.8 1.0 %partner_rows.1 = (bf16[48,128]{1,0:T(8,128)(2,1)S(1)}, bf16[48,128]{1,0:T(8,128)(2,1)S(1)}, bf16[48,128]{1,0:T(8,128)(2,1)S(1)}) custom-call(bf16[256,2176]{1,0:T(8,128)(2,1)S(1)} %get-tuple-element.13.keys_ref, bf16[2176,256]{1,0:T(8,128)(2,1)S(1)} %get-tuple-element.14.values_ref, s32[40,128]{1,0:T(8,128)S(1)} %get-tuple-element.15.limits_ref, ...), custom_call_target="tpu_custom_call" | custom-call | tf_op jit(solution)/shard_map/partner_rows/pallas_call | solution.py:260
  10.8 0.1 collective-permute-start.3
  10.9 2.6 %collective-permute-start.4 = (bf16[48,128]{1,0:T(8,128)(2,1)S(1)}, bf16[48,128]{1,0:T(8,128)(2,1)S(1)}, u32[]{:S(2)}, u32[]{:S(2)}) collective-permute-start(bf16[48,128]{1,0:T(8,128)(2,1)S(1)} %get-tuple-element.19), channel_id=1, source_target_pairs={{0,8},{4,12},{8,0},{12,4},{1,9},{5,13},{9,1},{13,5},{2,10},{6,14},... | collective-permute-start | bytes 36872 | tf_op jit(solution)/shard_map/ppermute | solution.py:202
  13.4 1.4 %collective-permute-start.5 = (bf16[48,128]{1,0:T(8,128)(2,1)S(1)}, bf16[48,128]{1,0:T(8,128)(2,1)S(1)}, u32[]{:S(2)}, u32[]{:S(2)}) collective-permute-start(bf16[48,128]{1,0:T(8,128)(2,1)S(1)} %get-tuple-element.20), channel_id=1, source_target_pairs={{0,12},{4,0},{8,4},{12,8},{1,13},{5,1},{9,5},{13,9},{2,14},{6,2},{... | collective-permute-start | bytes 36872 | tf_op jit(solution)/shard_map/ppermute | solution.py:202
  14.8 0.0 copy-done
  14.8 0.7 %own_rows.1 = (f32[40,128]{1,0:T(8,128)S(1)}, f32[40,128]{1,0:T(8,128)S(1)}) custom-call(bf16[256,2176]{1,0:T(8,128)(2,1)S(1)} %get-tuple-element.13.keys_ref, bf16[2176,256]{1,0:T(8,128)(2,1)S(1)} %get-tuple-element.14.values_ref, s32[40,128]{1,0:T(8,128)S(1)} %get-tuple-element.15.limits_ref, bf16[40,128]{1,0:T(8,128)(2,1)S(1)} %bitcast.29), custom_call_target="tpu_custom_call" | custom-call | tf_op jit(solution)/shard_map/own_rows/pallas_call | solution.py:246
  15.5 0.8 %collective-permute-done.3.refs_0_ = bf16[48,128]{1,0:T(8,128)(2,1)S(1)} collective-permute-done((bf16[48,128]{1,0:T(8,128)(2,1)S(1)}, bf16[48,128]{1,0:T(8,128)(2,1)S(1)}, u32[]{:S(2)}, u32[]{:S(2)}) %collective-permute-start.3) | collective-permute-done | bytes 12320 | tf_op jit(solution)/shard_map/ppermute | solution.py:202
  16.4 0.0 collective-permute-done.4.refs_1_
  16.4 0.8 %collective-permute-done.5.refs_2_ = bf16[48,128]{1,0:T(8,128)(2,1)S(1)} collective-permute-done((bf16[48,128]{1,0:T(8,128)(2,1)S(1)}, bf16[48,128]{1,0:T(8,128)(2,1)S(1)}, u32[]{:S(2)}, u32[]{:S(2)}) %collective-permute-start.5) | collective-permute-done | bytes 12320 | tf_op jit(solution)/shard_map/ppermute | solution.py:202
  17.1 0.8 %merge.1 = bf16[40,128]{1,0:T(8,128)(2,1)} custom-call(f32[40,128]{1,0:T(8,128)S(1)} %get-tuple-element.16.outputs_ref, f32[40,128]{1,0:T(8,128)S(1)} %get-tuple-element.17.stats_ref, bf16[48,128]{1,0:T(8,128)(2,1)S(1)} %collective-permute-done.3.refs_0_, bf16[48,128]{1,0:T(8,128)(2,1)S(1)} %collective-permute-done.4.refs_1_, ...), custom_call_target="tpu_custom_call" | custom-call | tf_op jit(solution)/shard_map/merge/pallas_call | solution.py:270
Async XLA Ops:
  0.0 8.2 %collective-permute-start.1 = (bf16[1,4,10,128]{3,1,2,0:T(4,128)(2,1)}, bf16[1,4,10,128]{3,1,2,0:T(4,128)(2,1)S(1)}, u32[]{:S(2)}, u32[]{:S(2)}) collective-permute-start(bf16[1,4,10,128]{3,1,2,0:T(4,128)(2,1)} %param.6), channel_id=1, source_target_pairs={{0,4},{4,8},{8,12},{12,0},{1,5},{5,9},{9,13},{13,1},{2,6},{6,10},{... | collective-permute-start | bytes 30728 | tf_op jit(solution)/shard_map/ppermute | solution.py:202
  3.0 5.1 %collective-permute-start.2 = (bf16[1,4,10,128]{3,1,2,0:T(4,128)(2,1)}, bf16[1,4,10,128]{3,1,2,0:T(4,128)(2,1)S(1)}, u32[]{:S(2)}, u32[]{:S(2)}) collective-permute-start(bf16[1,4,10,128]{3,1,2,0:T(4,128)(2,1)} %param.6), channel_id=1, source_target_pairs={{0,12},{4,0},{8,4},{12,8},{1,13},{5,1},{9,5},{13,9},{2,14},{6,2},{... | collective-permute-start | bytes 30728 | tf_op jit(solution)/shard_map/ppermute | solution.py:202
  5.1 4.8 %collective-permute-start = (bf16[1,4,10,128]{3,1,2,0:T(4,128)(2,1)}, bf16[1,4,10,128]{3,1,2,0:T(4,128)(2,1)S(1)}, u32[]{:S(2)}, u32[]{:S(2)}) collective-permute-start(bf16[1,4,10,128]{3,1,2,0:T(4,128)(2,1)} %param.6), channel_id=1, source_target_pairs={{0,8},{4,12},{8,0},{12,4},{1,9},{5,13},{9,1},{13,5},{2,10},{6,14},... | collective-permute-start | bytes 30728 | tf_op jit(solution)/shard_map/ppermute | solution.py:202
  9.8 5.0 %copy-start = (bf16[1,4,10,128]{3,1,2,0:T(4,128)(2,1)S(1)}, bf16[1,4,10,128]{3,1,2,0:T(4,128)(2,1)}, u32[]{:S(2)}) copy-start(bf16[1,4,10,128]{3,1,2,0:T(4,128)(2,1)} %param.6) | copy-start | bytes 30724
  10.8 5.5 %collective-permute-start.3 = (bf16[48,128]{1,0:T(8,128)(2,1)S(1)}, bf16[48,128]{1,0:T(8,128)(2,1)S(1)}, u32[]{:S(2)}, u32[]{:S(2)}) collective-permute-start(bf16[48,128]{1,0:T(8,128)(2,1)S(1)} %get-tuple-element.18), channel_id=1, source_target_pairs={{0,4},{4,8},{8,12},{12,0},{1,5},{5,9},{9,13},{13,1},{2,6},{6,10},{... | collective-permute-start | bytes 36872 | tf_op jit(solution)/shard_map/ppermute | solution.py:202
  10.9 5.5 %collective-permute-start.4 = (bf16[48,128]{1,0:T(8,128)(2,1)S(1)}, bf16[48,128]{1,0:T(8,128)(2,1)S(1)}, u32[]{:S(2)}, u32[]{:S(2)}) collective-permute-start(bf16[48,128]{1,0:T(8,128)(2,1)S(1)} %get-tuple-element.19), channel_id=1, source_target_pairs={{0,8},{4,12},{8,0},{12,4},{1,9},{5,13},{9,1},{13,5},{2,10},{6,14},... | collective-permute-start | bytes 36872 | tf_op jit(solution)/shard_map/ppermute | solution.py:202
  13.4 3.7 %collective-permute-start.5 = (bf16[48,128]{1,0:T(8,128)(2,1)S(1)}, bf16[48,128]{1,0:T(8,128)(2,1)S(1)}, u32[]{:S(2)}, u32[]{:S(2)}) collective-permute-start(bf16[48,128]{1,0:T(8,128)(2,1)S(1)} %get-tuple-element.20), channel_id=1, source_target_pairs={{0,12},{4,0},{8,4},{12,8},{1,13},{5,1},{9,5},{13,9},{2,14},{6,2},{... | collective-permute-start | bytes 36872 | tf_op jit(solution)/shard_map/ppermute | solution.py:202

commit v3 on v2

--- a/solution.py
+++ b/solution.py
@@ -172,8 +172,7 @@
         packet_ref[...] = pack(*[part[place * rows : (place + 1) * rows] for part in results])
 
 
-def merge_kernel(rows, outputs_ref, stats_ref, *refs):
-    packets, merged_ref = refs[:-1], refs[-1]
+def merge_parts(rows, outputs_ref, stats_ref, packets):
     stats = stats_ref[...]
     parts = [(outputs_ref[...], stats[:, 0:1], stats[:, 1:2])]
     for packet_ref in packets:
@@ -190,6 +189,20 @@
     factors = [jnp.exp2(top - highest) for _, top, _ in parts]
     total = sum(factor * part[2] for factor, part in zip(factors, parts))
     merged = sum(factor * part[0] for factor, part in zip(factors, parts))
+    return merged, highest, total
+
+
+def fold_kernel(rows, outputs_ref, stats_ref, *refs):
+    packets, (folded_ref, folded_stats_ref) = refs[:-2], refs[-2:]
+    merged, highest, total = merge_parts(rows, outputs_ref, stats_ref, packets)
+    folded_ref[...] = merged
+    lane = lax.broadcasted_iota(jnp.int32, folded_stats_ref.shape, 1)
+    folded_stats_ref[...] = jnp.where(lane == 0, highest, total)
+
+
+def merge_kernel(rows, outputs_ref, stats_ref, *refs):
+    packets, merged_ref = refs[:-1], refs[-1]
+    merged, _, total = merge_parts(rows, outputs_ref, stats_ref, packets)
     merged_ref[...] = (merged / total).astype(merged_ref.dtype)
 
 
@@ -266,6 +279,19 @@
             name="partner_rows",
         )(*prepared, *query_list)
 
+    def fold(outputs, stats, packets):
+        return pl.pallas_call(
+            functools.partial(fold_kernel, rows),
+            out_shape=(
+                jax.ShapeDtypeStruct((rows, width), jnp.float32),
+                jax.ShapeDtypeStruct((rows, lane_width), jnp.float32),
+            ),
+            in_specs=[vmem] * (2 + len(packets)),
+            out_specs=(vmem,) * 2,
+            compiler_params=pltpu.CompilerParams(vmem_limit_bytes=grant // 10),
+            name="fold",
+        )(outputs, stats, *packets)
+
     def merge(outputs, stats, packets):
         return pl.pallas_call(
             functools.partial(merge_kernel, rows),
@@ -276,14 +302,20 @@
             name="merge",
         )(outputs, stats, *packets)
 
+    offsets = list(range(1, workers))
     middle = workers // 2
-    offsets = [middle] + [offset for offset in range(1, workers) if offset != middle]
-    arrived = [as_rows(shift(queries, offset, workers)) for offset in offsets]
+    arrived = {offset: as_rows(shift(queries, offset, workers)) for offset in offsets}
     prepared = prepare()
-    sent = partners(prepared, arrived) if arrived else ()
-    packets = [shift(sent[offsets.index(workers - offset)], offset, workers) for offset in range(1, workers)]
+    sent = {}
+    for group in ([offset for offset in offsets if offset != middle], offsets[middle - 1 : middle]):
+        if group:
+            sent |= dict(zip(group, partners(prepared, [arrived[offset] for offset in group])))
+    packets = [shift(sent[workers - offset], offset, workers) for offset in offsets]
     outputs, stats = own(prepared, as_rows(queries))
-    merged = merge(outputs, stats, packets)
+    stages = [stage for stage in (packets[:1], packets[1:-1], packets[1:][-1:]) if stage]
+    for stage in stages[:-1]:
+        outputs, stats = fold(outputs, stats, stage)
+    merged = merge(outputs, stats, stages[-1] if stages else [])
     return merged.reshape(heads, steps, width).transpose(1, 0, 2)[None]
 
 

time: 18.1 us -> 17.6 us (0.972)
  waiting for transfers between devices: 3.29 us -> 0.88 us
  starting transfers between devices: 10 us -> 11 us
  Pallas kernels: 4.6 us -> 5.5 us
    ppermute x6, waiting for transfers between devices: 3.29 us -> 0.88 us  [shift(): lax.ppermute(shard, 'worker', [(i, (i + offset) % workers) for i in range...]
    ppermute x6, starting transfers between devices: 10 us -> 11 us  [shift(): lax.ppermute(shard, 'worker', [(i, (i + offset) % workers) for i in range...]
    pallas_call x1 -> x2, Pallas kernels: 0.97 us -> 1.56 us  [partners(): pl.pallas_call(functools.partial(partner_kernel, kv_local, steps, count),...]
    pallas_call x0 -> x2, Pallas kernels: none -> 0.36 us  [fold(): pl.pallas_call(functools.partial(fold_kernel, rows), out_shape=(jax.Shape...]
  transfers between devices with their start and end apart: 6 -> 6, of which waited for: 3 -> 2; matrix products, arithmetic and copies ran while one was open for 0% -> 0% of each run, Pallas kernels for 15% -> 27%
where the time goes in v3:
time: 17.6 us; the launch traced here: 17.5 us
  starting transfers between devices  11 us (62%)
  Pallas kernels  5.5 us (31%)
  waiting for transfers between devices  0.88 us (5%)
    ppermute x6, starting transfers between devices, shift(): lax.ppermute(shard, 'worker', [(i, (i + offset) % workers) for i in range...  11 us
    pallas_call x1, Pallas kernels, prepare(): pl.pallas_call(functools.partial(prepare_kernel, kv_local, steps, chunks)...  2.08 us
    pallas_call x2, Pallas kernels, partners(): pl.pallas_call(functools.partial(partner_kernel, kv_local, steps, count),...  1.56 us
    ppermute x6, waiting for transfers between devices, shift(): lax.ppermute(shard, 'worker', [(i, (i + offset) % workers) for i in range...  0.88 us
    pallas_call x1, Pallas kernels, merge(): pl.pallas_call(functools.partial(merge_kernel, rows), out_shape=jax.Shape...  0.79 us
    pallas_call x1, Pallas kernels, own(): pl.pallas_call(functools.partial(own_kernel, kv_local, steps), out_shape=...  0.71 us
    pallas_call x2, Pallas kernels, fold(): pl.pallas_call(functools.partial(fold_kernel, rows), out_shape=(jax.Shape...  0.36 us
  transfers between devices with their start and end apart: 6, of which 2 were waited for; matrix products, arithmetic and copies ran while one was open for 0% of the time, Pallas kernels for 27%

profile of v3, /device:TPU:0, one launch (start us, length us, event | category | flops | bytes accessed | tf_op | source)
XLA Modules:
  0.0 17.5 jit_solution(16582424002229431206)
XLA Ops:
  0.0 3.0 %collective-permute-start = (bf16[1,4,10,128]{3,1,2,0:T(4,128)(2,1)}, bf16[1,4,10,128]{3,1,2,0:T(4,128)(2,1)S(1)}, u32[]{:S(2)}, u32[]{:S(2)}) collective-permute-start(bf16[1,4,10,128]{3,1,2,0:T(4,128)(2,1)} %param.6), channel_id=1, source_target_pairs={{0,4},{4,8},{8,12},{12,0},{1,5},{5,9},{9,13},{13,1},{2,6},{6,10},{... | collective-permute-start | bytes 30728 | tf_op jit(solution)/shard_map/ppermute | solution.py:215
  3.0 2.0 %collective-permute-start.1 = (bf16[1,4,10,128]{3,1,2,0:T(4,128)(2,1)}, bf16[1,4,10,128]{3,1,2,0:T(4,128)(2,1)S(1)}, u32[]{:S(2)}, u32[]{:S(2)}) collective-permute-start(bf16[1,4,10,128]{3,1,2,0:T(4,128)(2,1)} %param.6), channel_id=1, source_target_pairs={{0,12},{4,0},{8,4},{12,8},{1,13},{5,1},{9,5},{13,9},{2,14},{6,2},{... | collective-permute-start | bytes 30728 | tf_op jit(solution)/shard_map/ppermute | solution.py:215
  5.1 1.0 %collective-permute-start.3 = (bf16[1,4,10,128]{3,1,2,0:T(4,128)(2,1)}, bf16[1,4,10,128]{3,1,2,0:T(4,128)(2,1)S(1)}, u32[]{:S(2)}, u32[]{:S(2)}) collective-permute-start(bf16[1,4,10,128]{3,1,2,0:T(4,128)(2,1)} %param.6), channel_id=1, source_target_pairs={{0,8},{4,12},{8,0},{12,4},{1,9},{5,13},{9,1},{13,5},{2,10},{6,14},... | collective-permute-start | bytes 30728 | tf_op jit(solution)/shard_map/ppermute | solution.py:215
  6.1 2.1 %prepare.1 = (bf16[256,2176]{1,0:T(8,128)(2,1)S(1)}, bf16[2176,256]{1,0:T(8,128)(2,1)S(1)}, s32[40,128]{1,0:T(8,128)S(1)}) custom-call(s32[1,4]{1,0:T(1,128)} %lengths_hbm.1, bf16[4096,128]{1,0:T(8,128)(2,1)} %bitcast.33, bf16[4096,128]{1,0:T(8,128)(2,1)} %bitcast.34, bf16[8,128]{1,0:T(8,128)(2,1)} %bitcast.35, bf16[8,128]{1,0:T(8,128)(2,1)} %bitcast.36), custom_call_target="tpu_custom_call" | custom-call | tf_op jit(solution)/shard_map/prepare/pallas_call | solution.py:229
  8.2 0.0 collective-permute-done
  8.2 0.0 collective-permute-done.1
  8.2 0.8 %partner_rows.2 = (bf16[48,128]{1,0:T(8,128)(2,1)S(1)}, bf16[48,128]{1,0:T(8,128)(2,1)S(1)}) custom-call(bf16[256,2176]{1,0:T(8,128)(2,1)S(1)} %get-tuple-element.16.keys_ref, bf16[2176,256]{1,0:T(8,128)(2,1)S(1)} %get-tuple-element.17.values_ref, s32[40,128]{1,0:T(8,128)S(1)} %get-tuple-element.18.limits_ref, bf16[40,128]{1,0:T(8,128)(2,1)S(1)} %bitcast.31, ...), custom_call_target="tpu_custom_call" | custom-call | tf_op jit(solution)/shard_map/partner_rows/pallas_call | solution.py:273
  9.0 1.6 %collective-permute-start.2 = (bf16[48,128]{1,0:T(8,128)(2,1)S(1)}, bf16[48,128]{1,0:T(8,128)(2,1)S(1)}, u32[]{:S(2)}, u32[]{:S(2)}) collective-permute-start(bf16[48,128]{1,0:T(8,128)(2,1)S(1)} %get-tuple-element.21), channel_id=1, source_target_pairs={{0,4},{4,8},{8,12},{12,0},{1,5},{5,9},{9,13},{13,1},{2,6},{6,10},{... | collective-permute-start | bytes 36872 | tf_op jit(solution)/shard_map/ppermute | solution.py:215
  10.6 0.0 collective-permute-done.3
  10.6 0.0 copy-start
  10.6 0.7 %partner_rows.3 = bf16[48,128]{1,0:T(8,128)(2,1)S(1)} custom-call(bf16[256,2176]{1,0:T(8,128)(2,1)S(1)} %get-tuple-element.16.keys_ref, bf16[2176,256]{1,0:T(8,128)(2,1)S(1)} %get-tuple-element.17.values_ref, s32[40,128]{1,0:T(8,128)S(1)} %get-tuple-element.18.limits_ref, bf16[40,128]{1,0:T(8,128)(2,1)S(1)} %bitcast.30), custom_call_target="tpu_custom_call" | custom-call | tf_op jit(solution)/shard_map/partner_rows/pallas_call | solution.py:273
  11.4 1.6 %collective-permute-start.4 = (bf16[48,128]{1,0:T(8,128)(2,1)S(1)}, bf16[48,128]{1,0:T(8,128)(2,1)S(1)}, u32[]{:S(2)}, u32[]{:S(2)}) collective-permute-start(bf16[48,128]{1,0:T(8,128)(2,1)S(1)} %partner_rows.3), channel_id=1, source_target_pairs={{0,8},{4,12},{8,0},{12,4},{1,9},{5,13},{9,1},{13,5},{2,10},{6,14},... | collective-permute-start | bytes 36872 | tf_op jit(solution)/shard_map/ppermute | solution.py:215
  13.0 1.7 %collective-permute-start.5 = (bf16[48,128]{1,0:T(8,128)(2,1)S(1)}, bf16[48,128]{1,0:T(8,128)(2,1)S(1)}, u32[]{:S(2)}, u32[]{:S(2)}) collective-permute-start(bf16[48,128]{1,0:T(8,128)(2,1)S(1)} %get-tuple-element.26), channel_id=1, source_target_pairs={{0,12},{4,0},{8,4},{12,8},{1,13},{5,1},{9,5},{13,9},{2,14},{6,2},{... | collective-permute-start | bytes 36872 | tf_op jit(solution)/shard_map/ppermute | solution.py:215
  14.7 0.0 copy-done
  14.7 0.7 %own_rows.1 = (f32[40,128]{1,0:T(8,128)S(1)}, f32[40,128]{1,0:T(8,128)S(1)}) custom-call(bf16[256,2176]{1,0:T(8,128)(2,1)S(1)} %get-tuple-element.16.keys_ref, bf16[2176,256]{1,0:T(8,128)(2,1)S(1)} %get-tuple-element.17.values_ref, s32[40,128]{1,0:T(8,128)S(1)} %get-tuple-element.18.limits_ref, bf16[40,128]{1,0:T(8,128)(2,1)S(1)} %bitcast.29), custom_call_target="tpu_custom_call" | custom-call | tf_op jit(solution)/shard_map/own_rows/pallas_call | solution.py:259
  15.4 0.0 collective-permute-done.2.refs_0_
  15.4 0.2 %fold.2 = (f32[40,128]{1,0:T(8,128)S(1)}, f32[40,128]{1,0:T(8,128)S(1)}) custom-call(f32[40,128]{1,0:T(8,128)S(1)} %get-tuple-element.19.outputs_ref, f32[40,128]{1,0:T(8,128)S(1)} %get-tuple-element.20.stats_ref, bf16[48,128]{1,0:T(8,128)(2,1)S(1)} %collective-permute-done.2.refs_0_), custom_call_target="tpu_custom_call" | custom-call | tf_op jit(solution)/shard_map/fold/pallas_call | solution.py:283
  15.6 0.4 %collective-permute-done.4.refs_0_ = bf16[48,128]{1,0:T(8,128)(2,1)S(1)} collective-permute-done((bf16[48,128]{1,0:T(8,128)(2,1)S(1)}, bf16[48,128]{1,0:T(8,128)(2,1)S(1)}, u32[]{:S(2)}, u32[]{:S(2)}) %collective-permute-start.4) | collective-permute-done | bytes 12320 | tf_op jit(solution)/shard_map/ppermute | solution.py:215
  16.0 0.2 %fold.3 = (f32[40,128]{1,0:T(8,128)S(1)}, f32[40,128]{1,0:T(8,128)S(1)}) custom-call(f32[40,128]{1,0:T(8,128)S(1)} %get-tuple-element.22.outputs_ref, f32[40,128]{1,0:T(8,128)S(1)} %get-tuple-element.23.stats_ref, bf16[48,128]{1,0:T(8,128)(2,1)S(1)} %collective-permute-done.4.refs_0_), custom_call_target="tpu_custom_call" | custom-call | tf_op jit(solution)/shard_map/fold/pallas_call | solution.py:283
  16.2 0.5 %collective-permute-done.5.refs_0_ = bf16[48,128]{1,0:T(8,128)(2,1)S(1)} collective-permute-done((bf16[48,128]{1,0:T(8,128)(2,1)S(1)}, bf16[48,128]{1,0:T(8,128)(2,1)S(1)}, u32[]{:S(2)}, u32[]{:S(2)}) %collective-permute-start.5) | collective-permute-done | bytes 12320 | tf_op jit(solution)/shard_map/ppermute | solution.py:215
  16.7 0.8 %merge.1 = bf16[40,128]{1,0:T(8,128)(2,1)} custom-call(f32[40,128]{1,0:T(8,128)S(1)} %get-tuple-element.24.outputs_ref, f32[40,128]{1,0:T(8,128)S(1)} %get-tuple-element.25.stats_ref, bf16[48,128]{1,0:T(8,128)(2,1)S(1)} %collective-permute-done.5.refs_0_), custom_call_target="tpu_custom_call" | custom-call | tf_op jit(solution)/shard_map/merge/pallas_call | solution.py:296
Async XLA Ops:
  0.0 8.2 %collective-permute-start = (bf16[1,4,10,128]{3,1,2,0:T(4,128)(2,1)}, bf16[1,4,10,128]{3,1,2,0:T(4,128)(2,1)S(1)}, u32[]{:S(2)}, u32[]{:S(2)}) collective-permute-start(bf16[1,4,10,128]{3,1,2,0:T(4,128)(2,1)} %param.6), channel_id=1, source_target_pairs={{0,4},{4,8},{8,12},{12,0},{1,5},{5,9},{9,13},{13,1},{2,6},{6,10},{... | collective-permute-start | bytes 30728 | tf_op jit(solution)/shard_map/ppermute | solution.py:215
  3.0 5.1 %collective-permute-start.1 = (bf16[1,4,10,128]{3,1,2,0:T(4,128)(2,1)}, bf16[1,4,10,128]{3,1,2,0:T(4,128)(2,1)S(1)}, u32[]{:S(2)}, u32[]{:S(2)}) collective-permute-start(bf16[1,4,10,128]{3,1,2,0:T(4,128)(2,1)} %param.6), channel_id=1, source_target_pairs={{0,12},{4,0},{8,4},{12,8},{1,13},{5,1},{9,5},{13,9},{2,14},{6,2},{... | collective-permute-start | bytes 30728 | tf_op jit(solution)/shard_map/ppermute | solution.py:215
  5.1 5.6 %collective-permute-start.3 = (bf16[1,4,10,128]{3,1,2,0:T(4,128)(2,1)}, bf16[1,4,10,128]{3,1,2,0:T(4,128)(2,1)S(1)}, u32[]{:S(2)}, u32[]{:S(2)}) collective-permute-start(bf16[1,4,10,128]{3,1,2,0:T(4,128)(2,1)} %param.6), channel_id=1, source_target_pairs={{0,8},{4,12},{8,0},{12,4},{1,9},{5,13},{9,1},{13,5},{2,10},{6,14},... | collective-permute-start | bytes 30728 | tf_op jit(solution)/shard_map/ppermute | solution.py:215
  9.0 6.4 %collective-permute-start.2 = (bf16[48,128]{1,0:T(8,128)(2,1)S(1)}, bf16[48,128]{1,0:T(8,128)(2,1)S(1)}, u32[]{:S(2)}, u32[]{:S(2)}) collective-permute-start(bf16[48,128]{1,0:T(8,128)(2,1)S(1)} %get-tuple-element.21), channel_id=1, source_target_pairs={{0,4},{4,8},{8,12},{12,0},{1,5},{5,9},{9,13},{13,1},{2,6},{6,10},{... | collective-permute-start | bytes 36872 | tf_op jit(solution)/shard_map/ppermute | solution.py:215
  10.6 4.1 %copy-start = (bf16[1,4,10,128]{3,1,2,0:T(4,128)(2,1)S(1)}, bf16[1,4,10,128]{3,1,2,0:T(4,128)(2,1)}, u32[]{:S(2)}) copy-start(bf16[1,4,10,128]{3,1,2,0:T(4,128)(2,1)} %param.6) | copy-start | bytes 30724
  11.4 4.7 %collective-permute-start.4 = (bf16[48,128]{1,0:T(8,128)(2,1)S(1)}, bf16[48,128]{1,0:T(8,128)(2,1)S(1)}, u32[]{:S(2)}, u32[]{:S(2)}) collective-permute-start(bf16[48,128]{1,0:T(8,128)(2,1)S(1)} %partner_rows.3), channel_id=1, source_target_pairs={{0,8},{4,12},{8,0},{12,4},{1,9},{5,13},{9,1},{13,5},{2,10},{6,14},... | collective-permute-start | bytes 36872 | tf_op jit(solution)/shard_map/ppermute | solution.py:215
  13.0 3.7 %collective-permute-start.5 = (bf16[48,128]{1,0:T(8,128)(2,1)S(1)}, bf16[48,128]{1,0:T(8,128)(2,1)S(1)}, u32[]{:S(2)}, u32[]{:S(2)}) collective-permute-start(bf16[48,128]{1,0:T(8,128)(2,1)S(1)} %get-tuple-element.26), channel_id=1, source_target_pairs={{0,12},{4,0},{8,4},{12,8},{1,13},{5,1},{9,5},{13,9},{2,14},{6,2},{... | collective-permute-start | bytes 36872 | tf_op jit(solution)/shard_map/ppermute | solution.py:215

commit v4 on v3

--- a/solution.py
+++ b/solution.py
@@ -28,17 +28,20 @@
     return pad_ref[...]
 
 
-def widen(shards, kv_local, steps):
-    count, (per_worker, width) = len(shards), shards[0].shape
+def stack(shards, kv_local, steps):
+    count, per_worker = len(shards), shards[0].shape[0]
     row = lax.broadcasted_iota(jnp.int32, (count * per_worker, 1), 0)
     head = row % per_worker // (per_worker // kv_local)
     rows = jnp.concatenate([shard.astype(jnp.float32) for shard in shards], axis=0)
-    wide = jnp.concatenate([jnp.where(head == k, rows, 0.0) for k in range(kv_local)], axis=1)
-    return wide.astype(jnp.bfloat16), row % steps, head
-
-
-def score(queries, keys, limit):
-    scores = jnp.dot(queries, keys, preferred_element_type=jnp.float32)
+    return rows.astype(jnp.bfloat16), row % steps, head
+
+
+def score(queries, head, keys, limit):
+    width = queries.shape[1]
+    scores = None
+    for k in range(keys.shape[0] // width):
+        part = jnp.dot(queries, keys[k * width : (k + 1) * width], preferred_element_type=jnp.float32)
+        scores = part if scores is None else jnp.where(head == k, part, scores)
     column = lax.broadcasted_iota(jnp.int32, scores.shape, 1)
     return jnp.where(column < limit, scores, masked_score)
 
@@ -49,14 +52,6 @@
     weights = [jnp.exp2(part * scale - top) for part in scores]
     total = sum(jnp.sum(part, axis=1, keepdims=True) for part in weights)
     return [part.astype(jnp.bfloat16) for part in weights], top, total
-
-
-def own_columns(both, head, kv_local):
-    width = both.shape[1] // kv_local
-    outputs = both[:, :width]
-    for k in range(1, kv_local):
-        outputs = jnp.where(head == k, both[:, k * width : (k + 1) * width], outputs)
-    return outputs
 
 
 def to_lanes(column):
@@ -107,6 +102,11 @@
     ]
     for copy in small + fetch[0] + fetch[1]:
         copy.start()
+    for i in range(chunks):
+        fetch[0][i].wait()
+        part, columns = pl.ds(i * size, size), pl.ds(i * span, span)
+        for k, picked in enumerate(pick_head(raw_keys_ref.at[part], wide_ref.at[0, part], kv_local)):
+            keys_ref[pl.ds(k * width, width), columns] = picked.astype(jnp.bfloat16).T
     for copy in small:
         copy.wait()
     step = lax.broadcasted_iota(jnp.int32, limits_ref.shape, 0) % steps
@@ -119,11 +119,6 @@
     keys_ref[:, pl.ds(slots, lane_width)] = fresh_keys.astype(jnp.bfloat16).T
     values_ref[pl.ds(slots, lane_width), :] = fresh_values.astype(jnp.bfloat16)
     for i in range(chunks):
-        fetch[0][i].wait()
-        part, columns = pl.ds(i * size, size), pl.ds(i * span, span)
-        for k, picked in enumerate(pick_head(raw_keys_ref.at[part], wide_ref.at[0, part], kv_local)):
-            keys_ref[pl.ds(k * width, width), columns] = picked.astype(jnp.bfloat16).T
-    for i in range(chunks):
         fetch[1][i].wait()
         part, lines = pl.ds(i * size, size), pl.ds(i * span, span)
         for k, picked in enumerate(pick_head(raw_values_ref.at[part], wide_ref.at[1, part], kv_local)):
@@ -134,11 +129,11 @@
     count, width = len(shards), shards[0].shape[1]
     slots = values_ref.shape[0] - lane_width
     scale = width ** (-0.5) * math.log2(math.e)
-    queries, step, head = widen(shards, kv_local, steps)
+    queries, step, head = stack(shards, kv_local, steps)
     limit = jnp.concatenate([limits_ref[:, 0:1]] * count, axis=0)
     scores = [
-        score(queries, keys_ref[:, pl.ds(0, slots)], limit),
-        score(queries, keys_ref[:, pl.ds(slots, lane_width)], step + 1 if own else step),
+        score(queries, head, keys_ref[:, pl.ds(0, slots)], limit),
+        score(queries, head, keys_ref[:, pl.ds(slots, lane_width)], step + 1 if own else step),
     ]
     weights, top, total = weigh(scores, scale)
     begins = (0, slots)
@@ -163,7 +158,7 @@
 
 
 def partner_kernel(kv_local, steps, count, keys_ref, values_ref, limits_ref, *refs):
-    shards, packets = refs[:count], refs[count:]
+    shards, packets = refs[-2 * count : -count], refs[-count:]
     rows = shards[0].shape[0]
     results = attend(
         [shard[...] for shard in shards], keys_ref, values_ref, limits_ref, kv_local, steps, False
@@ -268,16 +263,18 @@
             name="own_rows",
         )(*prepared, query_rows)
 
-    def partners(prepared, query_list):
+    def partners(prepared, query_list, earlier=()):
         count = len(query_list)
         return pl.pallas_call(
             functools.partial(partner_kernel, kv_local, steps, count),
             out_shape=(packet,) * count,
-            in_specs=[vmem] * (count + 3),
+            in_specs=[vmem] * 3
+            + [pl.BlockSpec(memory_space=pl.ANY)] * len(earlier)
+            + [vmem] * count,
             out_specs=(vmem,) * count,
             compiler_params=pltpu.CompilerParams(vmem_limit_bytes=grant),
             name="partner_rows",
-        )(*prepared, *query_list)
+        )(*prepared, *earlier, *query_list)
 
     def fold(outputs, stats, packets):
         return pl.pallas_call(
@@ -303,13 +300,13 @@
         )(outputs, stats, *packets)
 
     offsets = list(range(1, workers))
-    middle = workers // 2
     arrived = {offset: as_rows(shift(queries, offset, workers)) for offset in offsets}
     prepared = prepare()
     sent = {}
-    for group in ([offset for offset in offsets if offset != middle], offsets[middle - 1 : middle]):
+    for group, earlier in ((offsets[-1:], offsets[:-1][:1]), (offsets[:-1], [])):
         if group:
-            sent |= dict(zip(group, partners(prepared, [arrived[offset] for offset in group])))
+            packed = partners(prepared, [arrived[k] for k in group], [arrived[k] for k in earlier])
+            sent |= dict(zip(group, packed))
     packets = [shift(sent[workers - offset], offset, workers) for offset in offsets]
     outputs, stats = own(prepared, as_rows(queries))
     stages = [stage for stage in (packets[:1], packets[1:-1], packets[1:][-1:]) if stage]

time: 17.6 us -> 17.6 us (level)
  Pallas kernels: 5.5 us -> 5.32 us
  transfers between devices with their start and end apart: 6 -> 6, of which waited for: 2 -> 2; matrix products, arithmetic and copies ran while one was open for 0% -> 0% of each run, Pallas kernels for 27% -> 26%
where the time goes in v4:
time: 17.6 us; the launch traced here: 17.5 us
  starting transfers between devices  11 us (62%)
  Pallas kernels  5.32 us (30%)
  waiting for transfers between devices  1.02 us (6%)
    ppermute x6, starting transfers between devices, shift(): lax.ppermute(shard, 'worker', [(i, (i + offset) % workers) for i in range...  11 us
    pallas_call x1, Pallas kernels, prepare(): pl.pallas_call(functools.partial(prepare_kernel, kv_local, steps, chunks)...  1.96 us
    pallas_call x2, Pallas kernels, partners(): pl.pallas_call(functools.partial(partner_kernel, kv_local, steps, count),...  1.53 us
    ppermute x6, waiting for transfers between devices, shift(): lax.ppermute(shard, 'worker', [(i, (i + offset) % workers) for i in range...  1.02 us
    pallas_call x1, Pallas kernels, merge(): pl.pallas_call(functools.partial(merge_kernel, rows), out_shape=jax.Shape...  0.79 us
    pallas_call x1, Pallas kernels, own(): pl.pallas_call(functools.partial(own_kernel, kv_local, steps), out_shape=...  0.68 us
    pallas_call x2, Pallas kernels, fold(): pl.pallas_call(functools.partial(fold_kernel, rows), out_shape=(jax.Shape...  0.36 us
  transfers between devices with their start and end apart: 6, of which 2 were waited for; matrix products, arithmetic and copies ran while one was open for 0% of the time, Pallas kernels for 26%

profile of v4, /device:TPU:0, one launch (start us, length us, event | category | flops | bytes accessed | tf_op | source)
XLA Modules:
  0.0 17.5 jit_solution(7225733487205976802)
XLA Ops:
  0.0 3.0 %collective-permute-start = (bf16[1,4,10,128]{3,1,2,0:T(4,128)(2,1)}, bf16[1,4,10,128]{3,1,2,0:T(4,128)(2,1)S(1)}, u32[]{:S(2)}, u32[]{:S(2)}) collective-permute-start(bf16[1,4,10,128]{3,1,2,0:T(4,128)(2,1)} %param.6), channel_id=1, source_target_pairs={{0,4},{4,8},{8,12},{12,0},{1,5},{5,9},{9,13},{13,1},{2,6},{6,10},{... | collective-permute-start | bytes 30728 | tf_op jit(solution)/shard_map/ppermute | solution.py:210
  3.0 2.0 %collective-permute-start.1 = (bf16[1,4,10,128]{3,1,2,0:T(4,128)(2,1)}, bf16[1,4,10,128]{3,1,2,0:T(4,128)(2,1)S(1)}, u32[]{:S(2)}, u32[]{:S(2)}) collective-permute-start(bf16[1,4,10,128]{3,1,2,0:T(4,128)(2,1)} %param.6), channel_id=1, source_target_pairs={{0,12},{4,0},{8,4},{12,8},{1,13},{5,1},{9,5},{13,9},{2,14},{6,2},{... | collective-permute-start | bytes 30728 | tf_op jit(solution)/shard_map/ppermute | solution.py:210
  5.1 1.0 %collective-permute-start.3 = (bf16[1,4,10,128]{3,1,2,0:T(4,128)(2,1)}, bf16[1,4,10,128]{3,1,2,0:T(4,128)(2,1)S(1)}, u32[]{:S(2)}, u32[]{:S(2)}) collective-permute-start(bf16[1,4,10,128]{3,1,2,0:T(4,128)(2,1)} %param.6), channel_id=1, source_target_pairs={{0,8},{4,12},{8,0},{12,4},{1,9},{5,13},{9,1},{13,5},{2,10},{6,14},... | collective-permute-start | bytes 30728 | tf_op jit(solution)/shard_map/ppermute | solution.py:210
  6.1 2.0 %prepare.1 = (bf16[256,2176]{1,0:T(8,128)(2,1)S(1)}, bf16[2176,256]{1,0:T(8,128)(2,1)S(1)}, s32[40,128]{1,0:T(8,128)S(1)}) custom-call(s32[1,4]{1,0:T(1,128)} %lengths_hbm.1, bf16[4096,128]{1,0:T(8,128)(2,1)} %bitcast.34, bf16[4096,128]{1,0:T(8,128)(2,1)} %bitcast.35, bf16[8,128]{1,0:T(8,128)(2,1)} %bitcast.36, bf16[8,128]{1,0:T(8,128)(2,1)} %bitcast.37), custom_call_target="tpu_custom_call" | custom-call | tf_op jit(solution)/shard_map/prepare/pallas_call | solution.py:224
  8.0 0.0 collective-permute-done
  8.0 0.0 collective-permute-done.1
  8.1 0.7 %partner_rows.2 = bf16[48,128]{1,0:T(8,128)(2,1)S(1)} custom-call(bf16[256,2176]{1,0:T(8,128)(2,1)S(1)} %get-tuple-element.16.keys_ref, bf16[2176,256]{1,0:T(8,128)(2,1)S(1)} %get-tuple-element.17.values_ref, s32[40,128]{1,0:T(8,128)S(1)} %get-tuple-element.18.limits_ref, bf16[40,128]{1,0:T(8,128)(2,1)S(1)} %bitcast.29, bf16[40,128]{1,0:T(8,128)(2,1)S(1)} %bitcast.32), custom_call_target="tpu_custom_call" | custom-call | tf_op jit(solution)/shard_map/partner_rows/pallas_call | solution.py:268
  8.7 1.6 %collective-permute-start.2 = (bf16[48,128]{1,0:T(8,128)(2,1)S(1)}, bf16[48,128]{1,0:T(8,128)(2,1)S(1)}, u32[]{:S(2)}, u32[]{:S(2)}) collective-permute-start(bf16[48,128]{1,0:T(8,128)(2,1)S(1)} %partner_rows.2), channel_id=1, source_target_pairs={{0,4},{4,8},{8,12},{12,0},{1,5},{5,9},{9,13},{13,1},{2,6},{6,10},{... | collective-permute-start | bytes 36872 | tf_op jit(solution)/shard_map/ppermute | solution.py:210
  10.4 0.0 collective-permute-done.3
  10.4 0.0 copy-start
  10.4 0.8 %partner_rows.3 = (bf16[48,128]{1,0:T(8,128)(2,1)S(1)}, bf16[48,128]{1,0:T(8,128)(2,1)S(1)}) custom-call(bf16[256,2176]{1,0:T(8,128)(2,1)S(1)} %get-tuple-element.16.keys_ref, bf16[2176,256]{1,0:T(8,128)(2,1)S(1)} %get-tuple-element.17.values_ref, s32[40,128]{1,0:T(8,128)S(1)} %get-tuple-element.18.limits_ref, bf16[40,128]{1,0:T(8,128)(2,1)S(1)} %bitcast.30, ...), custom_call_target="tpu_custom_call" | custom-call | tf_op jit(solution)/shard_map/partner_rows/pallas_call | solution.py:268
  11.2 1.7 %collective-permute-start.4 = (bf16[48,128]{1,0:T(8,128)(2,1)S(1)}, bf16[48,128]{1,0:T(8,128)(2,1)S(1)}, u32[]{:S(2)}, u32[]{:S(2)}) collective-permute-start(bf16[48,128]{1,0:T(8,128)(2,1)S(1)} %get-tuple-element.23), channel_id=1, source_target_pairs={{0,8},{4,12},{8,0},{12,4},{1,9},{5,13},{9,1},{13,5},{2,10},{6,14},... | collective-permute-start | bytes 36872 | tf_op jit(solution)/shard_map/ppermute | solution.py:210
  13.0 1.6 %collective-permute-start.5 = (bf16[48,128]{1,0:T(8,128)(2,1)S(1)}, bf16[48,128]{1,0:T(8,128)(2,1)S(1)}, u32[]{:S(2)}, u32[]{:S(2)}) collective-permute-start(bf16[48,128]{1,0:T(8,128)(2,1)S(1)} %get-tuple-element.26), channel_id=1, source_target_pairs={{0,12},{4,0},{8,4},{12,8},{1,13},{5,1},{9,5},{13,9},{2,14},{6,2},{... | collective-permute-start | bytes 36872 | tf_op jit(solution)/shard_map/ppermute | solution.py:210
  14.6 0.0 copy-done
  14.6 0.7 %own_rows.1 = (f32[40,128]{1,0:T(8,128)S(1)}, f32[40,128]{1,0:T(8,128)S(1)}) custom-call(bf16[256,2176]{1,0:T(8,128)(2,1)S(1)} %get-tuple-element.16.keys_ref, bf16[2176,256]{1,0:T(8,128)(2,1)S(1)} %get-tuple-element.17.values_ref, s32[40,128]{1,0:T(8,128)S(1)} %get-tuple-element.18.limits_ref, bf16[40,128]{1,0:T(8,128)(2,1)S(1)} %bitcast.31), custom_call_target="tpu_custom_call" | custom-call | tf_op jit(solution)/shard_map/own_rows/pallas_call | solution.py:254
  15.3 0.0 collective-permute-done.2.refs_0_
  15.3 0.2 %fold.2 = (f32[40,128]{1,0:T(8,128)S(1)}, f32[40,128]{1,0:T(8,128)S(1)}) custom-call(f32[40,128]{1,0:T(8,128)S(1)} %get-tuple-element.19.outputs_ref, f32[40,128]{1,0:T(8,128)S(1)} %get-tuple-element.20.stats_ref, bf16[48,128]{1,0:T(8,128)(2,1)S(1)} %collective-permute-done.2.refs_0_), custom_call_target="tpu_custom_call" | custom-call | tf_op jit(solution)/shard_map/fold/pallas_call | solution.py:280
  15.5 0.4 %collective-permute-done.4.refs_0_ = bf16[48,128]{1,0:T(8,128)(2,1)S(1)} collective-permute-done((bf16[48,128]{1,0:T(8,128)(2,1)S(1)}, bf16[48,128]{1,0:T(8,128)(2,1)S(1)}, u32[]{:S(2)}, u32[]{:S(2)}) %collective-permute-start.4) | collective-permute-done | bytes 12320 | tf_op jit(solution)/shard_map/ppermute | solution.py:210
  15.9 0.2 %fold.3 = (f32[40,128]{1,0:T(8,128)S(1)}, f32[40,128]{1,0:T(8,128)S(1)}) custom-call(f32[40,128]{1,0:T(8,128)S(1)} %get-tuple-element.21.outputs_ref, f32[40,128]{1,0:T(8,128)S(1)} %get-tuple-element.22.stats_ref, bf16[48,128]{1,0:T(8,128)(2,1)S(1)} %collective-permute-done.4.refs_0_), custom_call_target="tpu_custom_call" | custom-call | tf_op jit(solution)/shard_map/fold/pallas_call | solution.py:280
  16.1 0.6 %collective-permute-done.5.refs_0_ = bf16[48,128]{1,0:T(8,128)(2,1)S(1)} collective-permute-done((bf16[48,128]{1,0:T(8,128)(2,1)S(1)}, bf16[48,128]{1,0:T(8,128)(2,1)S(1)}, u32[]{:S(2)}, u32[]{:S(2)}) %collective-permute-start.5) | collective-permute-done | bytes 12320 | tf_op jit(solution)/shard_map/ppermute | solution.py:210
  16.7 0.8 %merge.1 = bf16[40,128]{1,0:T(8,128)(2,1)} custom-call(f32[40,128]{1,0:T(8,128)S(1)} %get-tuple-element.24.outputs_ref, f32[40,128]{1,0:T(8,128)S(1)} %get-tuple-element.25.stats_ref, bf16[48,128]{1,0:T(8,128)(2,1)S(1)} %collective-permute-done.5.refs_0_), custom_call_target="tpu_custom_call" | custom-call | tf_op jit(solution)/shard_map/merge/pallas_call | solution.py:293
Async XLA Ops:
  0.0 8.0 %collective-permute-start = (bf16[1,4,10,128]{3,1,2,0:T(4,128)(2,1)}, bf16[1,4,10,128]{3,1,2,0:T(4,128)(2,1)S(1)}, u32[]{:S(2)}, u32[]{:S(2)}) collective-permute-start(bf16[1,4,10,128]{3,1,2,0:T(4,128)(2,1)} %param.6), channel_id=1, source_target_pairs={{0,4},{4,8},{8,12},{12,0},{1,5},{5,9},{9,13},{13,1},{2,6},{6,10},{... | collective-permute-start | bytes 30728 | tf_op jit(solution)/shard_map/ppermute | solution.py:210
  3.0 5.0 %collective-permute-start.1 = (bf16[1,4,10,128]{3,1,2,0:T(4,128)(2,1)}, bf16[1,4,10,128]{3,1,2,0:T(4,128)(2,1)S(1)}, u32[]{:S(2)}, u32[]{:S(2)}) collective-permute-start(bf16[1,4,10,128]{3,1,2,0:T(4,128)(2,1)} %param.6), channel_id=1, source_target_pairs={{0,12},{4,0},{8,4},{12,8},{1,13},{5,1},{9,5},{13,9},{2,14},{6,2},{... | collective-permute-start | bytes 30728 | tf_op jit(solution)/shard_map/ppermute | solution.py:210
  5.1 5.3 %collective-permute-start.3 = (bf16[1,4,10,128]{3,1,2,0:T(4,128)(2,1)}, bf16[1,4,10,128]{3,1,2,0:T(4,128)(2,1)S(1)}, u32[]{:S(2)}, u32[]{:S(2)}) collective-permute-start(bf16[1,4,10,128]{3,1,2,0:T(4,128)(2,1)} %param.6), channel_id=1, source_target_pairs={{0,8},{4,12},{8,0},{12,4},{1,9},{5,13},{9,1},{13,5},{2,10},{6,14},... | collective-permute-start | bytes 30728 | tf_op jit(solution)/shard_map/ppermute | solution.py:210
  8.7 6.5 %collective-permute-start.2 = (bf16[48,128]{1,0:T(8,128)(2,1)S(1)}, bf16[48,128]{1,0:T(8,128)(2,1)S(1)}, u32[]{:S(2)}, u32[]{:S(2)}) collective-permute-start(bf16[48,128]{1,0:T(8,128)(2,1)S(1)} %partner_rows.2), channel_id=1, source_target_pairs={{0,4},{4,8},{8,12},{12,0},{1,5},{5,9},{9,13},{13,1},{2,6},{6,10},{... | collective-permute-start | bytes 36872 | tf_op jit(solution)/shard_map/ppermute | solution.py:210
  10.4 4.2 %copy-start = (bf16[1,4,10,128]{3,1,2,0:T(4,128)(2,1)S(1)}, bf16[1,4,10,128]{3,1,2,0:T(4,128)(2,1)}, u32[]{:S(2)}) copy-start(bf16[1,4,10,128]{3,1,2,0:T(4,128)(2,1)} %param.6) | copy-start | bytes 30724
  11.2 4.7 %collective-permute-start.4 = (bf16[48,128]{1,0:T(8,128)(2,1)S(1)}, bf16[48,128]{1,0:T(8,128)(2,1)S(1)}, u32[]{:S(2)}, u32[]{:S(2)}) collective-permute-start(bf16[48,128]{1,0:T(8,128)(2,1)S(1)} %get-tuple-element.23), channel_id=1, source_target_pairs={{0,8},{4,12},{8,0},{12,4},{1,9},{5,13},{9,1},{13,5},{2,10},{6,14},... | collective-permute-start | bytes 36872 | tf_op jit(solution)/shard_map/ppermute | solution.py:210
  13.0 3.7 %collective-permute-start.5 = (bf16[48,128]{1,0:T(8,128)(2,1)S(1)}, bf16[48,128]{1,0:T(8,128)(2,1)S(1)}, u32[]{:S(2)}, u32[]{:S(2)}) collective-permute-start(bf16[48,128]{1,0:T(8,128)(2,1)S(1)} %get-tuple-element.26), channel_id=1, source_target_pairs={{0,12},{4,0},{8,4},{12,8},{1,13},{5,1},{9,5},{13,9},{2,14},{6,2},{... | collective-permute-start | bytes 36872 | tf_op jit(solution)/shard_map/ppermute | solution.py:210
